TPU v7x, 32 devices: a whole 2x2x4 slice. The times are simulated.
32 devices in a mesh: rep: 4 (over z), shard: 8 (over y, x, core).
Axes of the slice: x: 2, y: 2, z: 4, core: 2. Of those that a mesh axis runs over, the one named last changes fastest.
Arguments:
- tokens: bfloat16 [32768, 768], P(('rep', 'shard')), may hold values from -6 to 6
- word_counts: int32 [256], P(('rep', 'shard')), may hold values from 2 to 60
- region_counts: int32 [256], P(('rep', 'shard')), may hold values from 36 to 68
- task_labels: int32 [256], P(('rep', 'shard')), may hold values from 0 to 2
- masked_slots: int32 [256, 128], P(('rep', 'shard')), may hold values 0 or 1
- qkv_weight: bfloat16 [768, 2304], P('shard'), may hold values from -0.3125 to 0.3125
- query_bias: bfloat16 [768], P('shard'), may hold values from -3 to 3
- value_bias: bfloat16 [768], P('shard'), may hold values from -3 to 3
- out_weight: bfloat16 [768, 768], P('shard'), may hold values from -0.875 to 0.875
- out_bias: bfloat16 [768], P('shard'), may hold values from -3 to 3
- attn_gain: bfloat16 [768], P('shard'), may hold values from 0.5 to 1.5
- attn_shift: bfloat16 [768], P('shard'), may hold values from -3 to 3
- inner_weight: bfloat16 [768, 3072], P('shard'), may hold values from -0.21875 to 0.21875
- inner_bias: bfloat16 [3072], P('shard'), may hold values from -3 to 3
- back_weight: bfloat16 [3072, 768], P('shard'), may hold values from -0.109375 to 0.109375
- back_bias: bfloat16 [768], P('shard'), may hold values from -3 to 3
- ffn_gain: bfloat16 [768], P('shard'), may hold values from 0.5 to 1.5
- ffn_shift: bfloat16 [768], P('shard'), may hold values from -3 to 3
- cotangent: bfloat16 [32768, 768], P(('rep', 'shard')), may hold values from -6 to 6
Outputs:
- result: bfloat16 [32768, 768], P(('rep', 'shard'))
- input_grad: float32 [32768, 768], P(('rep', 'shard'))
- grad_qkv: float32 [768, 2304], P('shard')
- grad_query: float32 [768], P('shard')
- grad_value: float32 [768], P('shard')
- grad_proj: float32 [768, 768], P('shard')
- grad_pbias: float32 [768], P('shard')
- grad_again: float32 [768], P('shard')
- grad_ashift: float32 [768], P('shard')
- grad_inner: float32 [768, 3072], P('shard')
- grad_ibias: float32 [3072], P('shard')
- grad_back: float32 [3072, 768], P('shard')
- grad_bbias: float32 [768], P('shard')
- grad_fgain: float32 [768], P('shard')
- grad_fshift: float32 [768], P('shard')
All inputs are finite; a program needn't handle non-finite values. No bound on the sum of `masked_slots` on one device may be relied on, other than what follows from the above.
Results may differ from a plain program's by a relative error of at most 0.02.
Values may be sent and summed in bfloat16 or wider, within the bound.
No kernel may reach another device: no remote copies, remote signals or barrier semaphores. Data moves between devices by JAX's collectives and lax.ppermute only.
A program may use at most 192 MiB of HBM per device.

v0:
```python
import functools

import jax
import jax.numpy as jnp
from jax import lax
from jax.experimental import pallas as pl
from jax.experimental.pallas import tpu as pltpu
from jax.sharding import PartitionSpec as P

HEADS = 12
HEAD_DIM = 64
WORD_SLOTS = 60
CORE, XBIT, YBIT = 1, 2, 4
BLOCKS = 8
STEP = 256
LIVE = 192
WINDOW = 80
PART = 16
TOGETHER = 2
VMEM = 60 * 2**20
F32 = jnp.float32
BF16 = jnp.bfloat16


def mm(left, right):
    return jnp.dot(left, right, preferred_element_type=F32)


def mm_nt(left, right):
    return lax.dot_general(left, right, (((1,), (1,)), ((), ())), preferred_element_type=F32)


def mm_tn(left, right):
    return lax.dot_general(left, right, (((0,), (0,)), ((), ())), preferred_element_type=F32)


def norm_parts(value):
    mean = jnp.mean(value, -1, keepdims=True)
    centred = value - mean
    scale = lax.rsqrt(jnp.mean(centred * centred, -1, keepdims=True) + 1e-05)
    return centred * scale, scale


def norm_grad(grad, normed, scale):
    return scale * (
        grad
        - jnp.mean(grad, -1, keepdims=True)
        - normed * jnp.mean(grad * normed, -1, keepdims=True)
    )


def column_sum(value):
    return jnp.sum(value, 0, keepdims=True)


def start_pieces(pieces, offsets, scratch, sems, first=0, started=False):
    copies = []
    for j, piece in enumerate(pieces):
        start = pl.multiple_of(offsets[j], 16)
        source = piece.at[:, pl.ds(first, scratch.shape[1])]
        target = scratch.at[pl.ds(start, piece.shape[0]), :]
        copies.append(pltpu.make_async_copy(source, target, sems.at[j]))
        if not started:
            copies[-1].start()
    return copies


def stacked(block):
    lane = lax.broadcasted_iota(jnp.int32, block.shape, 1)
    zero = jnp.zeros_like(block)
    return jnp.concatenate(
        [jnp.where(lane < HEAD_DIM, block, zero), jnp.where(lane >= HEAD_DIM, block, zero)], 0
    )


def unstacked(block):
    rows = block.shape[0] // 2
    lane = lax.broadcasted_iota(jnp.int32, (rows, block.shape[1]), 1)
    return jnp.where(lane < HEAD_DIM, block[:rows], block[rows:])


def probabilities(queries, keys, valid):
    scores = jnp.where(valid, mm_nt(queries, keys), -1000000000.0)
    peak = jnp.max(scores, -1, keepdims=True)
    expo = jnp.exp(scores - peak)
    return expo * (1.0 / jnp.sum(expo, -1, keepdims=True))


def valid_slots(words, regions, seq):
    slot = lax.broadcasted_iota(jnp.int32, (1, seq), 1)
    return (slot < words) | ((slot >= WORD_SLOTS) & (slot < WORD_SLOTS + regions))


def selector(pos, start, seq):
    row = lax.broadcasted_iota(jnp.int32, (WINDOW, seq), 0) + start
    return jnp.where(row == pos, 1.0, 0.0).astype(BF16)


def window_start(base):
    return pl.multiple_of(base, PART)


def project_kernel(count, shard_rows, *refs):
    offsets = refs[0]
    pieces = refs[1 : 1 + count]
    tokens, qkv, vectors, bias, weights, sems = refs[1 + count :]
    width = tokens.shape[1]
    quarters = bias.shape[1] // width

    @pl.when(pl.program_id(0) == 0)
    def _():
        for copy in start_pieces(pieces, offsets, weights, sems):
            copy.wait()
        share = weights[:, 4 * width :].astype(F32)
        vectors[...] = share.T[: vectors.shape[0]]
        parts = []
        for s in range(width // shard_rows):
            for k in range(quarters):
                part = share[s * shard_rows : (s + 1) * shard_rows, 8 + k : 9 + k]
                parts.append(jnp.broadcast_to(part, (shard_rows, 8)))
        bias[...] = jnp.concatenate(parts, 0).T[:1]

    x = tokens[...]
    for part, row in ((0, 0), (1, None), (2, 1)):
        columns = slice(part * width, (part + 1) * width)
        value = mm(x, weights[:, columns])
        if row is not None:
            value = value + vectors[row : row + 1, :]
        qkv[:, columns] = value.astype(BF16)


def attend_kernel(count, seq, *refs):
    offsets, base, words, regions = refs[:4]
    pieces = refs[4 : 4 + count]
    tokens, cotangent, qkv, pos, vectors, hidden, compact, proj, mixed, sems = refs[4 + count :]
    width = tokens.shape[1]
    step = pl.program_id(0)

    @pl.when(step == 0)
    def _():
        copies = start_pieces(pieces, offsets, proj, sems, 3 * width)
        compact[...] = jnp.zeros_like(compact)
        for copy in copies:
            copy.wait()

    for k in range(STEP // seq):
        rows = slice(k * seq, (k + 1) * seq)
        pair = step * (STEP // seq) + k
        valid = valid_slots(words[pair], regions[pair], seq)
        for h in range(HEADS // 2):
            lanes = slice(h * 128, (h + 1) * 128)
            queries = stacked(qkv[rows, lanes] * HEAD_DIM ** (-0.5))
            keys = qkv[rows, width + h * 128 : width + (h + 1) * 128]
            values = qkv[rows, 2 * width + h * 128 : 2 * width + (h + 1) * 128]
            scores = jnp.where(valid, mm_nt(queries, keys), -1000000000.0)
            expo = jnp.exp(scores - jnp.max(scores, -1, keepdims=True)).astype(BF16)
            both = mm(expo, jnp.concatenate([values, jnp.ones_like(values)], 1))
            mixed[rows, lanes] = (unstacked(both[:, :128]) / unstacked(both[:, 128:])).astype(BF16)
    branch = mm(mixed[...], proj[...]) + vectors[2:3, :]
    normed, scale = norm_parts(tokens[...].astype(F32) + branch)
    value = normed * vectors[3:4, :] + vectors[4:5, :]
    hidden[...] = value
    high = scale.astype(BF16)
    rest = scale - high.astype(F32)
    middle = rest.astype(BF16)
    low = (rest - middle.astype(F32)).astype(BF16)
    lane = lax.broadcasted_iota(jnp.int32, (STEP, 128), 1)
    zero = jnp.zeros((STEP, 128), BF16)
    scales = jnp.where(lane == 0, high, jnp.where(lane == 1, middle, jnp.where(lane == 2, low, zero)))
    parts = (value.astype(BF16), normed.astype(BF16), mixed[...], cotangent[...], scales)
    for k in range(STEP // seq):
        pair = step * (STEP // seq) + k
        start = window_start(base[pair])
        chosen = selector(pos[pair], start, seq)
        at = 0
        for part in parts:
            columns = slice(at, at + part.shape[1])
            at += part.shape[1]
            got = mm(chosen, part[k * seq : (k + 1) * seq]).astype(BF16)
            compact[pl.ds(start, WINDOW), columns] = got


def gelu_parts(inner):
    cumul = 0.5 + 0.5 * lax.erf(inner * 0.7071067811865476)
    return inner * cumul, cumul


def live_inner_kernel(count, *refs):
    offsets, blocks = refs[:2]
    pieces = refs[2 : 2 + count]
    compact, bias, act_out, slope_out = refs[2 + count : 6 + count]
    weights, hidden, act, slope, sems, more = refs[6 + count :]
    width = hidden.shape[1]
    copies = start_pieces(pieces, offsets, weights, sems)
    count_live = blocks[0]

    def rows_of(b):
        return pl.ds(pl.multiple_of(b * LIVE, LIVE), LIVE)

    def load(b):
        return pltpu.make_async_copy(compact.at[rows_of(b), pl.ds(0, width)], hidden, more.at[0])

    load(0).start()
    for copy in copies:
        copy.wait()

    @pl.loop(0, count_live)
    def _(b):
        load(b).wait()
        x = hidden[...]
        for c in range(weights.shape[1] // width):
            columns = slice(c * width, (c + 1) * width)
            inner = mm(x, weights[:, columns]) + bias[:, columns]
            value, cumul = gelu_parts(inner)
            density = jnp.exp(-0.5 * inner * inner) * 0.3989422804014327
            act[:, columns] = value.astype(BF16)
            slope[:, columns] = (cumul + inner * density).astype(BF16)
        outs = [
            pltpu.make_async_copy(act, act_out.at[rows_of(b)], more.at[1]),
            pltpu.make_async_copy(slope, slope_out.at[rows_of(b)], more.at[2]),
        ]
        for copy in outs:
            copy.start()

        @pl.when(b + 1 < count_live)
        def _():
            load(b + 1).start()

        for copy in outs:
            copy.wait()


def ffn_kernel(counts, *refs):
    inner_offsets, back_offsets = refs[:2]
    inner_pieces = refs[2 : 2 + counts[0]]
    back_pieces = refs[2 + counts[0] : 2 + counts[0] + counts[1]]
    hidden, bias, vectors = refs[2 + sum(counts) : 5 + sum(counts)]
    result, inner, back, act, inner_sems, back_sems = refs[-6:]
    width = hidden.shape[1]
    step = pl.program_id(0)

    @pl.when(step == 0)
    def _():
        copies = start_pieces(inner_pieces, inner_offsets, inner, inner_sems)
        start_pieces(back_pieces, back_offsets, back, back_sems)
        for copy in copies:
            copy.wait()

    x = hidden[...]
    low = x.astype(BF16)
    for c in range(inner.shape[1] // width):
        columns = slice(c * width, (c + 1) * width)
        value = mm(low, inner[:, columns]) + bias[:, columns]
        act[:, columns] = gelu_parts(value)[0].astype(BF16)

    @pl.when(step == 0)
    def _():
        for copy in start_pieces(back_pieces, back_offsets, back, back_sems, started=True):
            copy.wait()

    second = mm(act[...], back[...]) + vectors[5:6, :]
    normed, _ = norm_parts(x + second)
    result[...] = (normed * vectors[6:7, :] + vectors[7:8, :]).astype(BF16)


def rows_of(b):
    return pl.ds(pl.multiple_of(b * LIVE, LIVE), LIVE)


def load_live(count_live, pairs, sems):
    def copies(b):
        here = rows_of(b)
        return [
            pltpu.make_async_copy(source(here), target.at[here], sems.at[j])
            for j, (source, target) in enumerate(pairs)
        ]

    for copy in copies(0):
        copy.start()

    def finish():
        for copy in copies(0):
            copy.wait()

        @pl.loop(1, count_live)
        def _(b):
            later = copies(b)
            for copy in later:
                copy.start()
            for copy in later:
                copy.wait()

    return finish


def store_live(count_live, pairs, sems):
    def copies(b):
        here = rows_of(b)
        return [
            pltpu.make_async_copy(source.at[here], target.at[here], sems.at[j])
            for j, (source, target) in enumerate(pairs)
        ]

    for copy in copies(0):
        copy.start()

    def finish():
        for copy in copies(0):
            copy.wait()

        @pl.loop(1, count_live)
        def _(b):
            later = copies(b)
            for copy in later:
                copy.start()
            for copy in later:
                copy.wait()

    return finish


def ffn_back_kernel(counts, *refs):
    inner_offsets, back_offsets, order, blocks = refs[:4]
    inner_pieces = refs[4 : 4 + counts[0]]
    back_pieces = refs[4 + counts[0] : 4 + sum(counts)]
    refs = refs[4 + sum(counts) :]
    compact_hbm, act_hbm, slope_hbm, vectors = refs[:4]
    keep_back, send_back, keep_inner, send_inner, d_hidden_out, sums, inner_sum = refs[4:11]
    back, inner, hidden, cotangent, act, slope, d_second, d_inner, d_hidden = refs[11:20]
    total, out_back, out_inner, turned, ordered, inner_sems, back_sems, more = refs[20:]
    width = inner.shape[0]
    size = inner.shape[1] // BLOCKS
    quarters = inner.shape[1] // width
    rows = width // BLOCKS
    half = BLOCKS // 2
    first = slice(0, LIVE)
    count_live = blocks[0]

    def live_copies(b):
        here = rows_of(b)
        return [
            pltpu.make_async_copy(compact_hbm.at[here, pl.ds(0, width)], hidden.at[here], more.at[0]),
            pltpu.make_async_copy(
                compact_hbm.at[here, pl.ds(3 * width, width)], cotangent.at[here], more.at[1]
            ),
            pltpu.make_async_copy(act_hbm.at[here], act.at[here], more.at[2]),
            pltpu.make_async_copy(slope_hbm.at[here], slope.at[here], more.at[3]),
        ]

    now = live_copies(0)
    for copy in now:
        copy.start()
    back_copies = start_pieces(back_pieces, back_offsets, back, back_sems)
    inner_copies = start_pieces(inner_pieces, inner_offsets, inner, inner_sems)
    sums[...] = jnp.zeros_like(sums)
    inner_sum[...] = jnp.zeros_like(inner_sum)
    for copy in now:
        copy.wait()

    @pl.loop(1, count_live)
    def _(b):
        later = live_copies(b)
        for copy in later:
            copy.start()
        for copy in later:
            copy.wait()

    for copy in back_copies:
        copy.wait()

    @pl.loop(0, count_live)
    def _(b):
        here = rows_of(b)
        second = mm(act[here, :], back[...]) + vectors[5:6, :]
        normed, scale = norm_parts(hidden[here, :].astype(F32) + second)
        d_out = cotangent[here, :].astype(F32)
        sums[6:7, :] += column_sum(d_out * normed)
        sums[7:8, :] += column_sum(d_out)
        d_r2 = norm_grad(d_out * vectors[6:7, :], normed, scale)
        low = d_r2.astype(BF16)
        d_second[here, :] = low
        sums[5:6, :] += column_sum(low.astype(F32))
        d_hidden[here, :] = d_r2

    single = count_live == 1
    outs = []
    for i in range(BLOCKS):
        chunk = pl.ds(pl.multiple_of(order[i] * size, 128), size)

        @pl.when(single)
        def _():
            out_back[i] = mm_tn(act[first, chunk], d_second[first, :]).astype(BF16)

        @pl.when(jnp.logical_not(single))
        def _():
            total[:size, :] = mm_tn(act[first, chunk], d_second[first, :])

            @pl.loop(1, count_live)
            def _(b):
                here = rows_of(b)
                total[:size, :] += mm_tn(act[here, chunk], d_second[here, :])

            out_back[i] = total[:size, :].astype(BF16)

        target = keep_back.at[i] if i < half else send_back.at[i - half]
        outs.append(pltpu.make_async_copy(out_back.at[i], target, more.at[4 + i]))
        outs[-1].start()
    for copy in inner_copies:
        copy.wait()

    @pl.loop(0, count_live)
    def _(b):
        here = rows_of(b)
        grad = d_second[here, :]
        for c in range(quarters):
            columns = slice(c * width, (c + 1) * width)
            d_act = mm_nt(grad, back[columns, :])
            low = (d_act * slope[here, columns].astype(F32)).astype(BF16)
            d_inner[here, columns] = low
            inner_sum[:, columns] += column_sum(low.astype(F32))
            d_hidden[here, :] += mm_nt(low, inner[:, columns])

    def hidden_copy(b):
        return pltpu.make_async_copy(
            d_hidden.at[rows_of(b)], d_hidden_out.at[rows_of(b)], more.at[0]
        )

    hidden_copy(0).start()

    @pl.loop(0, count_live)
    def _(b):
        here = rows_of(b)
        turned[...] = hidden[here, :].T
        for i in range(BLOCKS):
            start = pl.multiple_of(order[i] * rows, 16)
            ordered[b, i * rows : (i + 1) * rows, :] = turned[pl.ds(start, rows), :]

    for c in range(quarters):
        columns = slice(c * width, (c + 1) * width)
        target = slice(c * rows, (c + 1) * rows)

        @pl.when(single)
        def _():
            value = mm(ordered[0], d_inner[first, columns]).astype(BF16)
            for i in range(BLOCKS):
                out_inner[i, target, :] = value[i * rows : (i + 1) * rows, :]

        @pl.when(jnp.logical_not(single))
        def _():
            total[...] = mm(ordered[0], d_inner[first, columns])

            @pl.loop(1, count_live)
            def _(b):
                total[...] += mm(ordered[b], d_inner[rows_of(b), columns])

            for i in range(BLOCKS):
                out_inner[i, target, :] = total[i * rows : (i + 1) * rows, :].astype(BF16)

        for j, out in enumerate((keep_inner, send_inner)):
            blocks_out = pl.ds(j * half, half)
            part = pl.ds(c * rows, rows)
            source = out_inner.at[blocks_out, part]
            outs.append(pltpu.make_async_copy(source, out.at[:, part], more.at[12 + 2 * c + j]))
            outs[-1].start()
    hidden_copy(0).wait()

    @pl.loop(1, count_live)
    def _(b):
        hidden_copy(b).start()
        hidden_copy(b).wait()

    for copy in outs:
        copy.wait()


def by_head(block):
    lane = lax.broadcasted_iota(jnp.int32, block.shape, 1) // HEAD_DIM
    zero = jnp.zeros_like(block)
    return jnp.concatenate([jnp.where(lane == h, block, zero) for h in range(HEADS)], 0)


def from_heads(block):
    rows = block.shape[0] // HEADS
    lane = lax.broadcasted_iota(jnp.int32, (rows, 128), 1)
    parts = []
    for h in range(HEADS // 2):
        lanes = slice(h * 128, (h + 1) * 128)
        left = block[2 * h * rows : (2 * h + 1) * rows, lanes]
        right = block[(2 * h + 1) * rows : (2 * h + 2) * rows, lanes]
        parts.append(jnp.where(lane < HEAD_DIM, left, right))
    return jnp.concatenate(parts, 1)


def attend_back_kernel(count, seq, shard_rows, *refs):
    offsets, order, base, words, regions, blocks = refs[:6]
    pieces = refs[6 : 6 + count]
    refs = refs[6 + count :]
    compact, d_hidden_hbm, qkv_hbm, tokens_hbm, vectors, ffn_sums, inner_sum, pos = refs[:8]
    d_qkv_out, d_r1_out, keep_out, send_out = refs[8:12]
    weights, normed_in, mixed, scales, d_hidden, qkv, tokens, d_r1, d_mixed = refs[12:21]
    d_query, d_keys, d_values, d_qkv, total, out, sums = refs[21:28]
    turned, mixed_turned, tokens_turned, sems, more = refs[28:]
    width = weights.shape[0]
    rows = width // BLOCKS
    half = BLOCKS // 2
    pairs = pos.shape[0]
    count_live = blocks[0]

    loads = [
        (lambda here: compact.at[here, pl.ds(width, width)], normed_in),
        (lambda here: compact.at[here, pl.ds(2 * width, width)], mixed),
        (lambda here: compact.at[here, pl.ds(4 * width, 128)], scales),
        (lambda here: d_hidden_hbm.at[here], d_hidden),
    ]
    loaded = load_live(count_live, loads, more)
    weight_copies = start_pieces(pieces, offsets, weights, sems, 3 * width)
    qkv_copy = pltpu.make_async_copy(qkv_hbm, qkv, more.at[4])
    tokens_copy = pltpu.make_async_copy(tokens_hbm, tokens, more.at[5])
    qkv_copy.start()
    tokens_copy.start()
    d_r1[...] = jnp.zeros_like(d_r1)
    sums[...] = ffn_sums[...]
    loaded()
    for copy in weight_copies:
        copy.wait()

    @pl.loop(0, count_live)
    def _(b):
        here = rows_of(b)
        grad = d_hidden[here, :]
        normed = normed_in[here, :].astype(F32)
        scale = jnp.sum(scales[here, :].astype(F32), -1, keepdims=True)
        sums[3:4, :] += column_sum(grad * normed)
        sums[4:5, :] += column_sum(grad)
        low = norm_grad(grad * vectors[3:4, :], normed, scale).astype(BF16)
        sums[2:3, :] += column_sum(low.astype(F32))
        d_r1[here, :] = low
        d_mixed[here, :] = mm_nt(low, weights[...]).astype(BF16)

    def in_order(source, target):
        turned[:, : source.shape[0]] = source.T
        for i in range(BLOCKS):
            start = pl.multiple_of(order[i] * rows, 16)
            target[i * rows : (i + 1) * rows, :] = turned[pl.ds(start, rows), : source.shape[0]]

    outs = []

    def spread(value, first, size):
        low = value.astype(BF16)
        for i in range(BLOCKS):
            out[i, :, first : first + size] = low[i * rows : (i + 1) * rows, :size]
        columns = pl.ds(first, size)
        for j, target in enumerate((keep_out, send_out)):
            source = out.at[pl.ds(j * half, half), :, columns]
            sem = more.at[6 + len(outs)]
            outs.append(pltpu.make_async_copy(source, target.at[:, :, columns], sem))
            outs[-1].start()

    in_order(mixed[:LIVE, :], mixed_turned)

    @pl.when(count_live == 1)
    def _():
        total[...] = mm(mixed_turned[...], d_r1[:LIVE, :])

    @pl.when(count_live > 1)
    def _():
        total[...] = mm(mixed_turned[...], d_r1[:LIVE, :])

        @pl.loop(1, count_live)
        def _(b):
            here = rows_of(b)
            in_order(mixed[here, :], mixed_turned)
            total[...] += mm(mixed_turned[...], d_r1[here, :])

    spread(total[...], 3 * width, width)
    tokens_copy.wait()
    in_order(tokens[...], tokens_turned)
    qkv_copy.wait()

    def pair_part(pair, b):
        mine = pl.ds(pl.multiple_of(pair * seq, seq), seq)
        valid = valid_slots(words[pair], regions[pair], seq)
        first = pl.multiple_of(base[pair] + b * PART, PART)
        row = lax.broadcasted_iota(jnp.int32, (PART, seq), 0) + first
        chosen = jnp.where(row == pos[pair], 1.0, 0.0).astype(BF16)
        live_query = mm(chosen, qkv[mine, :width]).astype(BF16) * HEAD_DIM ** (-0.5)
        queries = by_head(live_query)
        grad = d_mixed[pl.ds(first, PART), :]
        row = lax.broadcasted_iota(jnp.int32, grad.shape, 0) + first
        grad = by_head(jnp.where(row < base[pair + 1], grad, jnp.zeros_like(grad)))
        keys = qkv[mine, width : 2 * width]
        probs = probabilities(queries, keys, valid)
        d_probs = mm_nt(grad, qkv[mine, 2 * width :])
        inside = jnp.sum(d_probs * probs, -1, keepdims=True)
        d_scores = (probs * (d_probs - inside)).astype(BF16)
        part = (from_heads(mm(d_scores, keys)) * HEAD_DIM ** (-0.5)).astype(BF16)
        return mm_tn(chosen, part), mm_tn(d_scores, queries), mm_tn(probs.astype(BF16), grad)

    @pl.loop(0, pairs // TOGETHER)
    def _(step):
        group = [step * TOGETHER + k for k in range(TOGETHER)]
        trips = (base[group[0] + 1] - base[group[0]]) // PART
        for pair in group[1:]:
            trips = jnp.maximum(trips, (base[pair + 1] - base[pair]) // PART)
        for k, pair in enumerate(group):
            for ref, value in zip((d_query, d_keys, d_values), pair_part(pair, 0)):
                ref[k] = value

        @pl.loop(1, trips)
        def _(b):
            for k, pair in enumerate(group):
                for ref, value in zip((d_query, d_keys, d_values), pair_part(pair, b)):
                    ref[k] += value

        for k, pair in enumerate(group):
            mine = pl.ds(pl.multiple_of(pair * seq, seq), seq)
            for part, ref in enumerate((d_query, d_keys, d_values)):
                low = ref[k].astype(BF16)
                d_qkv[mine, part * width : (part + 1) * width] = low
                if part != 1:
                    row = 0 if part == 0 else 1
                    sums[row : row + 1, :] += column_sum(low.astype(F32))

    column_form = jnp.broadcast_to(inner_sum[...], (8, inner_sum.shape[1])).T
    quarters = inner_sum.shape[1] // width
    block = jnp.concatenate([sums[...], jnp.zeros((128 - sums.shape[0], width), F32)], 0).T
    lane = lax.broadcasted_iota(jnp.int32, block.shape, 1)
    for k in range(quarters):
        starts = [(s * quarters + k) * shard_rows for s in range(width // shard_rows)]
        column = jnp.concatenate([column_form[s : s + shard_rows, :1] for s in starts], 0)
        block = jnp.where(lane == 8 + k, column, block)
    total[:, :128] = block
    spread(
        jnp.concatenate(
            [total[pl.ds(pl.multiple_of(order[i] * rows, 8), rows), :128] for i in range(BLOCKS)], 0
        ),
        4 * width,
        128,
    )
    for part in range(3):
        columns = slice(part * width, (part + 1) * width)
        spread(mm(tokens_turned[...], d_qkv[:, columns]), part * width, width)

    outs += [
        pltpu.make_async_copy(d_qkv, d_qkv_out, more.at[6 + len(outs)]),
        pltpu.make_async_copy(d_r1, d_r1_out, more.at[7 + len(outs)]),
    ]
    outs[-2].start()
    outs[-1].start()
    for copy in outs:
        copy.wait()


def input_grad_kernel(count, seq, *refs):
    offsets, base = refs[:2]
    pieces = refs[2 : 2 + count]
    d_qkv, d_r1, pos, out, weights, sems = refs[2 + count :]
    step = pl.program_id(0)

    @pl.when(step == 0)
    def _():
        for copy in start_pieces(pieces, offsets, weights, sems):
            copy.wait()

    value = mm_nt(d_qkv[...], weights[...])
    for k in range(STEP // seq):
        pair = step * (STEP // seq) + k
        start = window_start(base[pair])
        chosen = selector(pos[pair], start, seq)
        rows = slice(k * seq, (k + 1) * seq)
        out[rows, :] = value[rows] + mm_tn(chosen, d_r1[pl.ds(start, WINDOW), :])


def swap(value, bit):
    return lax.ppermute(value, "shard", [(i, i ^ bit) for i in range(8)])


def after(value, *others):
    return lax.optimization_barrier((value,) + others)[0]


def far_swap(by_x, by_y):
    half = by_x.shape[0] // 2
    return swap(by_y[:half], XBIT), swap(by_x[half:], YBIT)


def near_and_far(mine, by_x, by_y, by_both):
    far = XBIT | YBIT
    half = mine.shape[0] // 2
    near = [(mine, 0, 0), (by_x, XBIT, 0), (by_y, YBIT, 0)]
    return near + [(by_both[0], far, 0), (by_both[1], far, half)]


def with_core(pieces, others):
    return pieces + [(v, key | CORE, row) for v, (_, key, row) in zip(others, pieces)]


class Sum:
    def __init__(self, keep, send, early=False):
        self.keep, self.early = keep, early
        self.got = swap(send, CORE)
        self.extra = None
        z = lax.axis_index("rep")
        self.ends = (z == 0) | (z == 3)

    def wait(self, names, others):
        values = tuple(getattr(self, name) for name in names)
        got = lax.optimization_barrier(values + tuple(others))
        for name, value in zip(names, got):
            setattr(self, name, value)

    def chip(self, block, bottom):
        if self.early:
            half = self.mine.shape[1] // 2
            rows = slice(half, None) if bottom else slice(0, half)
            return self.mine[block, rows].astype(F32) + self.extra[block, rows].astype(F32)
        half = self.keep.shape[1] // 2
        rows = slice(half, None) if bottom else slice(0, half)
        return self.keep[block, rows].astype(F32) + self.got[block, rows].astype(F32)

    def rep_early(self, *others):
        self.wait(("keep", "got"), others)
        half = self.keep.shape[1] // 2
        a = self.keep[:, :half].astype(F32) + self.got[:, :half].astype(F32)
        b = self.keep[:, half:].astype(F32) + self.got[:, half:].astype(F32)
        sent = jnp.where(self.ends, b, a).astype(BF16)
        self.mine = jnp.where(self.ends, a, b).astype(BF16)
        self.extra = lax.ppermute(sent, "rep", PAIRS)
        return (sent,)

    def near(self, *others):
        self.wait(("mine", "extra") if self.early else ("keep", "got"), others)
        sent = self.chip(slice(1, 3), False).astype(BF16), self.chip(slice(2, 4), True).astype(BF16)
        self.got_a, self.got_b = swap(sent[0], XBIT), swap(sent[1], YBIT)
        return sent

    def far(self, *others):
        self.wait(("got_a", "got_b"), others)
        send_a = (self.chip(3, False) + self.got_a[1].astype(F32)).astype(BF16)
        send_b = (self.chip(1, True) + self.got_b[0].astype(F32)).astype(BF16)
        self.far_a, self.far_b = swap(send_a, YBIT), swap(send_b, XBIT)
        return send_a, send_b

    def halves(self):
        a = self.chip(0, False) + self.got_a[0].astype(F32) + self.far_a.astype(F32)
        b = self.chip(0, True) + self.got_b[1].astype(F32) + self.far_b.astype(F32)
        return a, b

    def rep_first(self, *others):
        self.wait(("far_a", "far_b"), others)
        a, b = self.halves()
        sent = jnp.where(self.ends, b, a).astype(BF16)
        self.total = jnp.where(self.ends, a, b).astype(BF16)
        self.across = lax.ppermute(sent, "rep", PAIRS)
        return (sent,)

    def rep_second(self, *others):
        if self.early:
            self.wait(("far_a", "far_b"), others)
            self.total = jnp.concatenate(self.halves(), 0).astype(BF16)
        else:
            self.wait(("across",), others)
            self.total = (self.total.astype(F32) + self.across.astype(F32)).astype(BF16)
        self.across = lax.ppermute(self.total, "rep", ACROSS)
        return (self.total,)

    def rep_third(self, *others):
        self.wait(("across",), others)
        self.low = (self.total.astype(F32) + self.across.astype(F32)).astype(BF16)
        self.other = lax.ppermute(self.low, "rep", PAIRS)
        return (self.low,)

    def done(self):
        top = jnp.where(self.ends, self.low, self.other)
        bottom = jnp.where(self.ends, self.other, self.low)
        return jnp.concatenate([top, bottom], 0).astype(F32)


PAIRS = [(0, 1), (1, 0), (2, 3), (3, 2)]
ACROSS = [(0, 3), (3, 0), (1, 2), (2, 1)]


def whole(shape, dtype=None):
    del dtype
    return pl.BlockSpec(shape, lambda *_: (0,) * len(shape))


def steps(width):
    return pl.BlockSpec((STEP, width), lambda i: (i, 0))


SCALARS = pl.BlockSpec(memory_space=pltpu.SMEM)
ANYWHERE = pl.BlockSpec(memory_space=pl.ANY)


def shape_of(*dims, dtype=BF16):
    return jax.ShapeDtypeStruct(dims, dtype)


def params():
    return pltpu.CompilerParams(vmem_limit_bytes=VMEM)


def cost(time):
    return pl.CostEstimate(flops=int(time * 1e8), bytes_accessed=0, transcendentals=0)


def local(
    tokens,
    word_counts,
    region_counts,
    task_labels,
    masked_slots,
    qkv_weight,
    query_bias,
    value_bias,
    out_weight,
    out_bias,
    attn_gain,
    attn_shift,
    inner_weight,
    inner_bias,
    back_weight,
    back_bias,
    ffn_gain,
    ffn_shift,
    cotangent,
    *,
    shards,
    reps,
):
    pairs = word_counts.shape[0]
    count, width = tokens.shape
    hidden = back_weight.shape[0] * shards
    seq = count // pairs
    grid = (count // STEP,)
    cap = -(-pairs * WINDOW // LIVE) * LIVE
    cube = shards == 8 and reps == 4
    rows = width // shards
    me = lax.axis_index("shard")

    slots = jnp.arange(seq, dtype=jnp.int32)[None, :]
    words = word_counts[:, None]
    in_regions = (slots >= WORD_SLOTS) & (slots < WORD_SLOTS + region_counts[:, None])
    picked = masked_slots == 1
    labels = task_labels[:, None]
    live = (
        (labels == 0) & picked & (slots >= 1) & (slots < words)
        | (labels == 1) & picked & in_regions
        | (labels == 2) & (slots == 0)
    )
    live_count = jnp.sum(live.astype(jnp.int32), 1)
    taken = (live_count + PART - 1) // PART * PART
    base = jnp.concatenate([jnp.zeros((1,), jnp.int32), jnp.cumsum(taken)])
    rank = jnp.cumsum(live.astype(jnp.int32), 1) - 1 + base[:-1, None]
    pos = jnp.where(live, rank, -1).reshape(pairs, 1, seq)
    blocks = jnp.maximum(1, (base[-1:] + LIVE - 1) // LIVE)

    vectors = jnp.stack(
        [query_bias, value_bias, out_bias, attn_gain, attn_shift, back_bias, ffn_gain, ffn_shift]
        + [inner_bias[k * rows : (k + 1) * rows] for k in range(hidden // width)],
        1,
    )
    vectors = jnp.pad(vectors, ((0, 0), (0, 128 - vectors.shape[1])))
    attn_shard = jnp.concatenate([qkv_weight, out_weight, vectors], 1)
    def offsets(size):
        if not cube:
            return jnp.zeros((1,), jnp.int32)
        keys = jnp.array([0, XBIT, YBIT, XBIT | YBIT, XBIT | YBIT], jnp.int32)
        starts = jnp.array([0, 0, 0, 0, size // 2], jnp.int32)
        return jnp.concatenate([(keys ^ me) * size + starts, (keys ^ me ^ CORE) * size + starts])

    small_offsets, back_offsets = offsets(rows), offsets(back_weight.shape[0])
    order = jnp.arange(BLOCKS, dtype=jnp.int32)
    if cube:
        order = jnp.array([0, 2, 6, 4, 1, 3, 7, 5], jnp.int32) ^ me
    indices = (base, pos, blocks, small_offsets, back_offsets, order)
    if cube:
        attn_x, attn_y = swap(attn_shard, XBIT), swap(attn_shard, YBIT)
        own = [swap(v, CORE) for v in (attn_shard, inner_weight, back_weight)]
        near = lax.optimization_barrier((attn_x, attn_y, inner_weight, indices, *own))
        attn_x, attn_y, inner_weight, indices, *own = near
        attn_far = far_swap(attn_x, attn_y)
        inner_x, inner_y = swap(inner_weight, XBIT), swap(inner_weight, YBIT)
        attn_core = swap(attn_x, CORE), swap(attn_y, CORE)
        attn_far, attn_core, back_weight = lax.optimization_barrier((attn_far, attn_core, back_weight))
        back_x, back_y = swap(back_weight, XBIT), swap(back_weight, YBIT)
        attn = near_and_far(attn_shard, attn_x, attn_y, attn_far)
        attn_core = (own[0],) + attn_core + tuple(swap(v, CORE) for v in attn_far)
        attn = with_core(attn, attn_core)
    else:
        attn, inner, back = (
            [(lax.all_gather(v, "shard", axis=0, tiled=True), 0, 0)]
            for v in (attn_shard, inner_weight, back_weight)
        )
    base, pos, blocks, small_offsets, back_offsets, order = indices

    columns = 4 * width + 128
    attn_count = len(attn)
    attn_offsets, attn_pieces = small_offsets, [v for v, _, _ in attn]
    qkv, vector_rows, inner_bias_full = pl.pallas_call(
        functools.partial(project_kernel, attn_count, rows),
        grid=grid,
        in_specs=[SCALARS] + [ANYWHERE] * attn_count + [steps(width)],
        out_specs=[steps(3 * width), whole((16, width)), whole((1, hidden))],
        out_shape=[
            shape_of(count, 3 * width),
            shape_of(16, width, dtype=F32),
            shape_of(1, hidden, dtype=F32),
        ],
        scratch_shapes=[
            pltpu.VMEM((width, columns), BF16),
            pltpu.SemaphoreType.DMA((attn_count,)),
        ],
        compiler_params=params(),
        cost_estimate=cost(9),
        name="project",
    )(attn_offsets, *attn_pieces, tokens)
    if cube:
        inner_x, inner_y, qkv = lax.optimization_barrier((inner_x, inner_y, qkv))
        inner_far = far_swap(inner_x, inner_y)
    hidden1, compact = pl.pallas_call(
        functools.partial(attend_kernel, attn_count, seq),
        grid=grid,
        in_specs=[SCALARS] * 4
        + [ANYWHERE] * attn_count
        + [steps(width), steps(width), steps(3 * width), whole((pairs, 1, seq)), whole((16, width))],
        out_specs=[steps(width), whole((cap, columns))],
        out_shape=[shape_of(count, width, dtype=F32), shape_of(cap, columns)],
        scratch_shapes=[
            pltpu.VMEM((width, width), BF16),
            pltpu.VMEM((STEP, width), BF16),
            pltpu.SemaphoreType.DMA((attn_count,)),
        ],
        compiler_params=params(),
        cost_estimate=cost(14),
        name="attend",
    )(
        attn_offsets,
        base,
        word_counts,
        region_counts,
        *attn_pieces,
        tokens,
        cotangent,
        qkv,
        pos,
        vector_rows,
    )

    if cube:
        inner_x, inner_y, inner_far, back_x, back_y = lax.optimization_barrier(
            (inner_x, inner_y, inner_far, back_x, back_y, hidden1)
        )[:5]
        back_far = far_swap(back_x, back_y)
        inner_core = [own[1]] + [swap(v, CORE) for v in (inner_x, inner_y) + inner_far]
        inner = with_core(near_and_far(inner_weight, inner_x, inner_y, inner_far), inner_core)
    inner_count = len(inner)
    inner_offsets, inner_pieces = small_offsets, [v for v, _, _ in inner]
    in_vmem = pl.BlockSpec(memory_space=pltpu.VMEM)
    live_act, live_slope = pl.pallas_call(
        functools.partial(live_inner_kernel, inner_count),
        in_specs=[SCALARS] * 2 + [ANYWHERE] * (inner_count + 1) + [in_vmem],
        out_specs=[ANYWHERE] * 2,
        out_shape=[shape_of(cap, hidden)] * 2,
        scratch_shapes=[
            pltpu.VMEM((width, hidden), BF16),
            pltpu.VMEM((LIVE, width), BF16),
            pltpu.VMEM((LIVE, hidden), BF16),
            pltpu.VMEM((LIVE, hidden), BF16),
            pltpu.SemaphoreType.DMA((inner_count,)),
            pltpu.SemaphoreType.DMA((3,)),
        ],
        compiler_params=params(),
        cost_estimate=cost(6),
        name="live_inner",
    )(inner_offsets, blocks, *inner_pieces, compact, inner_bias_full)

    if cube:
        back_far, back_near, live_act = lax.optimization_barrier((back_far, (back_x, back_y), live_act))
        back_core = [own[2]] + [swap(v, CORE) for v in back_near + back_far]
        back = with_core(near_and_far(back_weight, *back_near, back_far), back_core)
    back_count = len(back)
    back_pieces = [v for v, _, _ in back]

    half = BLOCKS // 2
    size = hidden // BLOCKS
    block = width // BLOCKS
    keep_back, send_back, keep_inner, send_inner, d_hidden1, sums, inner_sum = pl.pallas_call(
        functools.partial(ffn_back_kernel, (inner_count, back_count)),
        in_specs=[SCALARS] * 4 + [ANYWHERE] * (inner_count + back_count + 3) + [in_vmem],
        out_specs=[ANYWHERE] * 5 + [in_vmem] * 2,
        out_shape=[
            shape_of(half, size, width),
            shape_of(half, size, width),
            shape_of(half, size, width),
            shape_of(half, size, width),
            shape_of(cap, width, dtype=F32),
            shape_of(16, width, dtype=F32),
            shape_of(1, hidden, dtype=F32),
        ],
        scratch_shapes=[
            pltpu.VMEM((hidden, width), BF16),
            pltpu.VMEM((width, hidden), BF16),
            pltpu.VMEM((cap, width), BF16),
            pltpu.VMEM((cap, width), BF16),
            pltpu.VMEM((cap, hidden), BF16),
            pltpu.VMEM((cap, hidden), BF16),
            pltpu.VMEM((cap, width), BF16),
            pltpu.VMEM((cap, hidden), BF16),
            pltpu.VMEM((cap, width), F32),
            pltpu.VMEM((width, width), F32),
            pltpu.VMEM((BLOCKS, size, width), BF16),
            pltpu.VMEM((BLOCKS, size, width), BF16),
            pltpu.VMEM((width, LIVE), BF16),
            pltpu.VMEM((cap // LIVE, width, LIVE), BF16),
            pltpu.SemaphoreType.DMA((inner_count,)),
            pltpu.SemaphoreType.DMA((back_count,)),
            pltpu.SemaphoreType.DMA((12 + 2 * hidden // width,)),
        ],
        compiler_params=params(),
        cost_estimate=cost(13),
        name="ffn_back",
    )(
        inner_offsets,
        back_offsets,
        order,
        blocks,
        *inner_pieces,
        *back_pieces,
        compact,
        live_act,
        live_slope,
        vector_rows,
    )

    if cube:
        back_total = Sum(keep_back, send_back)
        inner_total = Sum(keep_inner, send_inner, early=True)

    d_qkv, d_r1, keep_attn, send_attn = pl.pallas_call(
        functools.partial(attend_back_kernel, attn_count, seq, rows),
        in_specs=[SCALARS] * 6 + [ANYWHERE] * (attn_count + 4) + [in_vmem] * 4,
        out_specs=[ANYWHERE] * 4,
        out_shape=[
            shape_of(count, 3 * width),
            shape_of(cap, width),
            shape_of(half, block, columns),
            shape_of(half, block, columns),
        ],
        scratch_shapes=[
            pltpu.VMEM((width, width), BF16),
            pltpu.VMEM((cap, width), BF16),
            pltpu.VMEM((cap, width), BF16),
            pltpu.VMEM((cap, 128), BF16),
            pltpu.VMEM((cap, width), F32),
            pltpu.VMEM((count, 3 * width), BF16),
            pltpu.VMEM((count, width), BF16),
            pltpu.VMEM((cap, width), BF16),
            pltpu.VMEM((cap, width), BF16),
            pltpu.VMEM((TOGETHER, seq, width), F32),
            pltpu.VMEM((TOGETHER, seq, width), F32),
            pltpu.VMEM((TOGETHER, seq, width), F32),
            pltpu.VMEM((count, 3 * width), BF16),
            pltpu.VMEM((width, width), F32),
            pltpu.VMEM((BLOCKS, block, columns), BF16),
            pltpu.VMEM((16, width), F32),
            pltpu.VMEM((width, count), BF16),
            pltpu.VMEM((width, LIVE), BF16),
            pltpu.VMEM((width, count), BF16),
            pltpu.SemaphoreType.DMA((attn_count,)),
            pltpu.SemaphoreType.DMA((16 + count // STEP,)),
        ],
        compiler_params=params(),
        cost_estimate=cost(22),
        name="attend_back",
    )(
        attn_offsets,
        order,
        base,
        word_counts,
        region_counts,
        blocks,
        *attn_pieces,
        compact,
        d_hidden1,
        qkv,
        tokens,
        vector_rows,
        sums,
        inner_sum,
        pos,
    )

    def later(shift):
        return lambda i: (i + shift, 0)

    def ffn(first, x, *done):
        return pl.pallas_call(
            functools.partial(ffn_kernel, (inner_count, back_count)),
            grid=(grid[0] // 2,),
            in_specs=[SCALARS] * 2
            + [ANYWHERE] * (inner_count + back_count)
            + [pl.BlockSpec((STEP, width), later(first)), whole((1, hidden)), whole((16, width))]
            + [ANYWHERE] * len(done),
            out_specs=pl.BlockSpec((STEP, width), later(first)),
            out_shape=shape_of(count, width),
            input_output_aliases={5 + inner_count + back_count: 0} if done else {},
            scratch_shapes=[
                pltpu.VMEM((width, hidden), BF16),
                pltpu.VMEM((hidden, width), BF16),
                pltpu.VMEM((STEP, hidden), BF16),
                pltpu.SemaphoreType.DMA((inner_count,)),
                pltpu.SemaphoreType.DMA((back_count,)),
            ],
            compiler_params=params(),
            cost_estimate=cost(11),
            name="ffn",
        )(
            inner_offsets,
            back_offsets,
            *inner_pieces,
            *back_pieces,
            x,
            inner_bias_full,
            vector_rows,
            *done,
        )

    x = hidden1
    if cube:
        sent = back_total.near(d_r1)
        sent += inner_total.rep_early(*sent)
        attn_total = Sum(keep_attn, send_attn)
        sent += attn_total.near(*sent)
        x = after(hidden1, *sent)
    result = ffn(0, x)
    if cube:
        sent = back_total.far(result)
        sent += attn_total.far(*sent)
        sent += back_total.rep_first(*sent)
        sent += inner_total.near(*sent)
        sent += attn_total.rep_first(*sent)
        sent += back_total.rep_second(*sent)
        sent += inner_total.far(*sent)
        d_qkv = after(d_qkv, *sent)

    input_grad = pl.pallas_call(
        functools.partial(input_grad_kernel, attn_count, seq),
        grid=grid,
        in_specs=[SCALARS] * 2
        + [ANYWHERE] * attn_count
        + [steps(3 * width), whole((cap, width)), whole((pairs, 1, seq))],
        out_specs=steps(width),
        out_shape=shape_of(count, width, dtype=F32),
        scratch_shapes=[
            pltpu.VMEM((width, 3 * width), BF16),
            pltpu.SemaphoreType.DMA((attn_count,)),
        ],
        compiler_params=params(),
        cost_estimate=cost(9),
        name="input_grad",
    )(attn_offsets, base, *attn_pieces, d_qkv, d_r1, pos)

    if cube:
        sent = attn_total.rep_second(input_grad)
        sent += back_total.rep_third(*sent)
        x = after(hidden1, *sent)
    result = ffn(grid[0] // 2, x, result)
    if cube:
        sent = inner_total.rep_second(result)

    quarters = hidden // width
    if cube:
        attn_total.rep_third(*sent)
        inner_total.rep_third()
        back_sum, inner_sum, attn_sum = (v.done() for v in (back_total, inner_total, attn_total))
        inner_sum = jnp.concatenate([inner_sum[c * block : (c + 1) * block] for c in range(quarters)], 1)
    else:
        back_grad = jnp.concatenate([keep_back, send_back]).reshape(hidden, width)
        inner_grad = jnp.concatenate([keep_inner, send_inner]).reshape(BLOCKS, quarters, block, width)
        inner_grad = inner_grad.transpose(0, 2, 1, 3).reshape(width, hidden)
        attn_grad = jnp.concatenate([keep_attn, send_attn]).reshape(width, columns)
        back_sum, inner_sum, attn_sum = (
            lax.psum(lax.psum_scatter(g, "shard", scatter_dimension=0, tiled=True), "rep").astype(F32)
            for g in (back_grad, inner_grad, attn_grad)
        )
    sums = attn_sum[:, 4 * width :].T
    return (
        result,
        input_grad,
        attn_sum[:, : 3 * width],
        sums[0],
        sums[1],
        attn_sum[:, 3 * width : 4 * width],
        sums[2],
        sums[3],
        sums[4],
        inner_sum,
        sums[8 : 8 + quarters].reshape(-1),
        back_sum,
        sums[5],
        sums[6],
        sums[7],
    )


def solution(mesh):
    rows, both, one = P(("rep", "shard"), None), P(("rep", "shard")), P("shard")
    matrix = P("shard", None)
    in_specs = (rows, both, both, both, rows, matrix, one, one, matrix, one, one, one)
    in_specs += (matrix, one, matrix, one, one, one, rows)
    out_specs = (rows, rows, matrix, one, one, matrix, one, one, one, matrix, one, matrix)
    out_specs += (one, one, one)
    sizes = dict(mesh.shape)

    def run(*args):
        return local(*args, shards=sizes["shard"], reps=sizes["rep"])

    return jax.shard_map(
        run, mesh=mesh, in_specs=in_specs, out_specs=out_specs, check_vma=False
    )
```

profile of v0, /device:TPU:0, one launch (start us, length us, event | category | flops | bytes accessed | tf_op | source)
XLA Modules:
  0.0 251.2 jit_solution(14438381499096389949)
XLA Ops:
  4.3 2.6 %collective-permute-start.1 = (bf16[96,3200]{1,0:T(8,128)(2,1)S(1)}, bf16[96,3200]{1,0:T(8,128)(2,1)S(1)}, u32[]{:S(2)}, u32[]{:S(2)}) collective-permute-start(bf16[96,3200]{1,0:T(8,128)(2,1)S(1)} %fusion.1.refs_1_.refs_4_.refs_6_.refs_2_), channel_id=1, source_target_pairs={{0,4},{1,5},{2,6},{3,7},{4,0},{5,1},{6,2},{7,3},{8,12},{9,13},{10,... | collective-permute-start | bytes 1843208 | tf_op jit(solution)/shard_map/ppermute | solution.py:675
  12.8 8.5 %collective-permute-done.1.refs_3_.refs_6_.refs_8_.refs_4_ = bf16[96,3200]{1,0:T(8,128)(2,1)S(1)} collective-permute-done((bf16[96,3200]{1,0:T(8,128)(2,1)S(1)}, bf16[96,3200]{1,0:T(8,128)(2,1)S(1)}, u32[]{:S(2)}, u32[]{:S(2)}) %collective-permute-start.1) | collective-permute-done | bytes 614432 | tf_op jit(solution)/shard_map/ppermute | solution.py:675
  25.4 7.2 %collective-permute-done.7.refs_4_.refs_7_.refs_9_.refs_5_ = bf16[48,3200]{1,0:T(8,128)(2,1)S(1)} collective-permute-done((bf16[48,3200]{1,0:T(8,128)(2,1)S(1)}, bf16[48,3200]{1,0:T(8,128)(2,1)S(1)}, u32[]{:S(2)}, u32[]{:S(2)}) %collective-permute-start.7) | collective-permute-done | bytes 307232 | tf_op jit(solution)/shard_map/ppermute | solution.py:675
  39.5 9.8 %project.1 = (bf16[1024,2304]{1,0:T(8,128)(2,1)}, f32[16,768]{1,0:T(8,128)}, f32[1,3072]{1,0:T(1,128)}) custom-call(s32[10]{0:T(128)} %get-tuple-element.91.refs_0_, bf16[96,3200]{1,0:T(8,128)(2,1)} %copy-done, bf16[96,3200]{1,0:T(8,128)(2,1)} %copy-done.2, bf16[96,3200]{1,0:T(8,128)(2,1)} %copy-done.1, bf16[48,3200]{1,0:T(8,128)(2,1)} %copy-done.13, ...), custom_call_target="tpu_custom_call" | custom-call | flops 900000000 | tf_op jit(solution)/shard_map/project/pallas_call | solution.py:901
  49.3 1.8 collective-permute-done.6.refs_4_.refs_6_
  53.9 17.0 %attend.1 = (f32[1024,768]{1,0:T(8,128)}, bf16[768,3200]{1,0:T(8,128)(2,1)}) custom-call(s32[10]{0:T(128)} %get-tuple-element.91.refs_0_, s32[9]{0:T(128)} %copy-done.33, s32[8]{0:T(128)} %refs_3_.3, s32[8]{0:T(128)} %refs_4_.2, bf16[96,3200]{1,0:T(8,128)(2,1)} %copy-done, bf16[96,3200]{1,0:T(8,128)(2,1)} %copy-done.2, bf16[96,3200]{1,0:T(8,128)(2,1)} %copy-done.1, ...), custom_call_target="tpu_custom_call" | custom-call | flops 1400000000 | tf_op jit(solution)/shard_map/attend/pallas_call | solution.py:922
  72.0 1.7 slice.251
  73.7 1.7 slice.252
  78.5 6.5 %live_inner.1 = (bf16[768,3072]{1,0:T(8,128)(2,1)}, bf16[768,3072]{1,0:T(8,128)(2,1)}) custom-call(s32[10]{0:T(128)} %get-tuple-element.91.refs_0_, s32[1]{0:T(128)S(6)} %max.3.refs_1_.refs_3_.refs_5_, bf16[96,3072]{1,0:T(8,128)(2,1)} %refs_2_.4, bf16[96,3072]{1,0:T(8,128)(2,1)} %copy-done.4, bf16[96,3072]{1,0:T(8,128)(2,1)} %copy-done.3, ...), custom_call_target="tpu_custom_call" | custom-call | flops 600000000 | tf_op jit(solution)/shard_map/live_inner/pallas_call | solution.py:961
  86.2 2.9 %collective-permute-done.25.refs_22_.refs_20_ = bf16[192,768]{1,0:T(8,128)(2,1)S(1)} collective-permute-done((bf16[192,768]{1,0:T(8,128)(2,1)}, bf16[192,768]{1,0:T(8,128)(2,1)S(1)}, u32[]{:S(2)}, u32[]{:S(2)}) %collective-permute-start.25) | collective-permute-done | bytes 294944 | tf_op jit(solution)/shard_map/ppermute | solution.py:675
  90.2 16.9 %ffn_back.1 = (bf16[4,384,768]{2,1,0:T(8,128)(2,1)}, bf16[4,384,768]{2,1,0:T(8,128)(2,1)}, bf16[4,384,768]{2,1,0:T(8,128)(2,1)}, bf16[4,384,768]{2,1,0:T(8,128)(...) custom-call(s32[10]{0:T(128)} %get-tuple-element.91.refs_0_, s32[10]{0:T(128)} %get-tuple-element.92.refs_1_, ...), custom_call_target="tpu_custom_call" | custom-call | flops 1300000000 | tf_op jit(solution)/shard_map/ffn_back/pallas_call | solution.py:989
  107.8 32.2 %attend_back.1 = (bf16[1024,2304]{1,0:T(8,128)(2,1)}, bf16[768,768]{1,0:T(8,128)(2,1)}, bf16[4,96,3200]{2,1,0:T(8,128)(2,1)}, bf16[4,96,3200]{2,1,0:T(8,128)(2,1)}) custom-call(s32[10]{0:T(128)} %get-tuple-element.91.refs_0_, s32[8]{0:T(128)} %broadcast_xor_fusion.refs_2_.refs_1_, s32[9]{0:T(128)} %copy-done.33, s32[8]{0:T(128)} %refs_3_.3, s32[8]{0:T(128)} %refs_4_.2, ...), custom_call_target="tpu_custom_call" | custom-call | flops 2200000000 | tf_op jit(solution)/shard_map/attend_back/pallas_call | solution.py:1041
  140.1 2.7 %add_convert_fusion.2 = (bf16[2,192,768]{2,1,0:T(8,128)(2,1)}, bf16[2,192,768]{2,1,0:T(8,128)(2,1)}) fusion(bf16[4,384,768]{2,1,0:T(8,128)(2,1)} %collective-permute-done.28, bf16[4,384,768]{2,1,0:T(8,128)(2,1)S(1)} %copy-done.21), kind=kLoop, calls=%fused_computation.9 | loop fusion | flops 2359296 | bytes 3538944 | tf_op jit(solution)/shard_map/convert_element_type | solution.py:733
  145.6 3.5 %select_convert_fusion = (bf16[4,192,768]{2,1,0:T(8,128)(2,1)S(1)}, bf16[4,192,768]{2,1,0:T(8,128)(2,1)}) fusion(pred[]{:T(512)S(6)} %or.13, bf16[4,384,768]{2,1,0:T(8,128)(2,1)} %collective-permute-done.29, bf16[4,384,768]{2,1,0:T(8,128)(2,1)S(1)} %copy-done.26), kind=kLoop, calls=%fused_computation | loop fusion | flops 5898240 | bytes 7077889 | tf_op jit(solution)/shard_map/convert_element_type | solution.py:727
  149.2 2.6 %add_convert_fusion = (bf16[2,48,3200]{2,1,0:T(8,128)(2,1)}, bf16[2,48,3200]{2,1,0:T(8,128)(2,1)}) fusion(bf16[4,96,3200]{2,1,0:T(8,128)(2,1)} %collective-permute-done.27, bf16[4,96,3200]{2,1,0:T(8,128)(2,1)S(1)} %copy-done.20), kind=kLoop, calls=%fused_computation.5 | loop fusion | flops 2457600 | bytes 3686400 | tf_op jit(solution)/shard_map/convert_element_type | solution.py:733
  153.0 1.6 collective-permute-start.38
  154.6 13.6 %ffn.2.refs_25_ = bf16[1024,768]{1,0:T(8,128)(2,1)} custom-call(s32[10]{0:T(128)} %get-tuple-element.91.refs_0_, s32[10]{0:T(128)} %get-tuple-element.92.refs_1_, bf16[96,3072]{1,0:T(8,128)(2,1)} %refs_2_.4, bf16[96,3072]{1,0:T(8,128)(2,1)} %copy-done.4, bf16[96,3072]{1,0:T(8,128)(2,1)} %copy-done.3, bf16[48,3072]{1,0:T(8,128)(2,1)} %copy-done.16, ...), custom_call_target="tpu_custom_call" | custom-call | flops 1100000000 | tf_op jit(solution)/shard_map/ffn/pallas_call | solution.py:1099
  168.2 1.6 fusion.5
  177.0 3.3 %collective-permute-done.37 = bf16[192,768]{1,0:T(8,128)(2,1)S(1)} collective-permute-done((bf16[192,768]{1,0:T(8,128)(2,1)S(1)}, bf16[192,768]{1,0:T(8,128)(2,1)S(1)}, u32[]{:S(2)}, u32[]{:S(2)}) %collective-permute-start.37) | collective-permute-done | bytes 294944 | tf_op jit(solution)/shard_map/ppermute | solution.py:675
  181.8 1.6 collective-permute-start.40
  186.7 1.8 select_convert_fusion.2
  188.6 1.7 collective-permute-start.39
  190.3 2.3 add_convert_fusion.10
  192.6 2.6 %collective-permute-start.43 = (bf16[192,768]{1,0:T(8,128)(2,1)}, bf16[192,768]{1,0:T(8,128)(2,1)}, u32[]{:S(2)}, u32[]{:S(2)}) collective-permute-start(bf16[192,768]{1,0:T(8,128)(2,1)} %add_convert_fusion.10), channel_id=1, source_target_pairs={{0,24},{24,0},{8,16},{16,8},{1,25},{25,1},{9,17},{17,9},{2,26},{26... | collective-permute-start | bytes 884744 | tf_op jit(solution)/shard_map/ppermute | solution.py:764
  195.9 1.9 fusion.9
  199.7 10.0 %input_grad.1 = f32[1024,768]{1,0:T(8,128)} custom-call(s32[10]{0:T(128)} %get-tuple-element.91.refs_0_, s32[9]{0:T(128)} %copy-done.33, bf16[96,3200]{1,0:T(8,128)(2,1)} %copy-done, bf16[96,3200]{1,0:T(8,128)(2,1)} %copy-done.2, bf16[96,3200]{1,0:T(8,128)(2,1)} %copy-done.1, bf16[48,3200]{1,0:T(8,128)(2,1)} %copy-done.13, bf16[48,3200]{1,0:T(8,128)(2,1)} %copy-done.14, ...), custom_call_target="tpu_custom_call" | custom-call | flops 900000000 | tf_op jit(solution)/shard_map/input_grad/pallas_call | solution.py:1148
  209.8 1.9 add_convert_fusion.5
  214.4 13.4 %ffn.3 = bf16[1024,768]{1,0:T(8,128)(2,1)} custom-call(s32[10]{0:T(128)} %get-tuple-element.91.refs_0_, s32[10]{0:T(128)} %get-tuple-element.92.refs_1_, bf16[96,3072]{1,0:T(8,128)(2,1)} %refs_2_.4, bf16[96,3072]{1,0:T(8,128)(2,1)} %copy-done.4, bf16[96,3072]{1,0:T(8,128)(2,1)} %copy-done.3, ...), custom_call_target="tpu_custom_call", output_to_operand_aliasing={{}: (25, {})} | custom-call | flops 1100000000 | tf_op jit(solution)/shard_map/ffn/pallas_call | solution.py:1099
  229.1 3.0 %collective-permute-start.48 = (bf16[192,768]{1,0:T(8,128)(2,1)S(1)}, bf16[192,768]{1,0:T(8,128)(2,1)S(1)}, u32[]{:S(2)}, u32[]{:S(2)}) collective-permute-start(bf16[192,768]{1,0:T(8,128)(2,1)S(1)} %pad_maximum_fusion.1), channel_id=1, source_target_pairs={{0,24},{24,0},{8,16},{16,8},{1,25},{25,1},{9,17},{17,9},{2,26},{26... | collective-permute-start | bytes 884744 | tf_op jit(solution)/shard_map/ppermute | solution.py:764
  234.4 5.8 %collective-permute-done.48 = bf16[192,768]{1,0:T(8,128)(2,1)S(1)} collective-permute-done((bf16[192,768]{1,0:T(8,128)(2,1)S(1)}, bf16[192,768]{1,0:T(8,128)(2,1)S(1)}, u32[]{:S(2)}, u32[]{:S(2)}) %collective-permute-start.48) | collective-permute-done | bytes 294944 | tf_op jit(solution)/shard_map/ppermute | solution.py:764
  240.2 1.8 collective-permute-start.49
  242.0 3.5 %collective-permute-done.47 = bf16[48,3200]{1,0:T(8,128)(2,1)S(1)} collective-permute-done((bf16[48,3200]{1,0:T(8,128)(2,1)S(1)}, bf16[48,3200]{1,0:T(8,128)(2,1)S(1)}, u32[]{:S(2)}, u32[]{:S(2)}) %collective-permute-start.47) | collective-permute-done | bytes 307232 | tf_op jit(solution)/shard_map/ppermute | solution.py:770
  (218 shorter events, 59.9 us)
Async XLA Ops:
  4.3 17.0 %collective-permute-start.1 = (bf16[96,3200]{1,0:T(8,128)(2,1)S(1)}, bf16[96,3200]{1,0:T(8,128)(2,1)S(1)}, u32[]{:S(2)}, u32[]{:S(2)}) collective-permute-start(bf16[96,3200]{1,0:T(8,128)(2,1)S(1)} %fusion.1.refs_1_.refs_4_.refs_6_.refs_2_), channel_id=1, source_target_pairs={{0,4},{1,5},{2,6},{3,7},{4,0},{5,1},{6,2},{7,3},{8,12},{9,13},{10,... | collective-permute-start | bytes 1843208 | tf_op jit(solution)/shard_map/ppermute | solution.py:675
  6.9 15.9 %collective-permute-start = (bf16[96,3200]{1,0:T(8,128)(2,1)S(1)}, bf16[96,3200]{1,0:T(8,128)(2,1)S(1)}, u32[]{:S(2)}, u32[]{:S(2)}) collective-permute-start(bf16[96,3200]{1,0:T(8,128)(2,1)S(1)} %fusion.1.refs_1_.refs_4_.refs_6_.refs_2_), channel_id=1, source_target_pairs={{0,2},{1,3},{2,0},{3,1},{4,6},{5,7},{6,4},{7,5},{8,10},{9,11},{10,... | collective-permute-start | bytes 1843208 | tf_op jit(solution)/shard_map/ppermute | solution.py:675
  22.8 11.0 %collective-permute-start.9 = (bf16[96,3200]{1,0:T(8,128)(2,1)S(1)}, bf16[96,3200]{1,0:T(8,128)(2,1)S(1)}, u32[]{:S(2)}, u32[]{:S(2)}) collective-permute-start(bf16[96,3200]{1,0:T(8,128)(2,1)S(1)} %collective-permute-done.refs_2_.refs_5_.refs_7_.refs_3_), channel_id=1, source_target_pairs={{0,1},{1,0},{2,3},{3,2},{4,5},{5,4},{6,7},{7,6},{8,9},{9,8},{10,11... | collective-permute-start | bytes 1843208 | tf_op jit(solution)/shard_map/ppermute | solution.py:675
  22.8 11.0 %collective-permute-start.10 = (bf16[96,3200]{1,0:T(8,128)(2,1)S(1)}, bf16[96,3200]{1,0:T(8,128)(2,1)S(1)}, u32[]{:S(2)}, u32[]{:S(2)}) collective-permute-start(bf16[96,3200]{1,0:T(8,128)(2,1)S(1)} %collective-permute-done.1.refs_3_.refs_6_.refs_8_.refs_4_), channel_id=1, source_target_pairs={{0,1},{1,0},{2,3},{3,2},{4,5},{5,4},{6,7},{7,6},{8,9},{9,8},{10,11... | collective-permute-start | bytes 1843208 | tf_op jit(solution)/shard_map/ppermute | solution.py:675
  34.7 16.4 %collective-permute-start.6 = (bf16[96,3072]{1,0:T(8,128)(2,1)}, bf16[96,3072]{1,0:T(8,128)(2,1)S(1)}, u32[]{:S(2)}, u32[]{:S(2)}) collective-permute-start(bf16[96,3072]{1,0:T(8,128)(2,1)} %refs_2_.4), channel_id=1, source_target_pairs={{0,4},{1,5},{2,6},{3,7},{4,0},{5,1},{6,2},{7,3},{8,12},{9,13},{10,... | collective-permute-start | bytes 1769480 | tf_op jit(solution)/shard_map/ppermute | solution.py:675
  35.2 16.5 %collective-permute-start.5 = (bf16[96,3072]{1,0:T(8,128)(2,1)}, bf16[96,3072]{1,0:T(8,128)(2,1)S(1)}, u32[]{:S(2)}, u32[]{:S(2)}) collective-permute-start(bf16[96,3072]{1,0:T(8,128)(2,1)} %refs_2_.4), channel_id=1, source_target_pairs={{0,2},{1,3},{2,0},{3,1},{4,6},{5,7},{6,4},{7,5},{8,10},{9,11},{10,... | collective-permute-start | bytes 1769480 | tf_op jit(solution)/shard_map/ppermute | solution.py:675
  35.7 35.2 %collective-permute-start.16 = (bf16[384,768]{1,0:T(8,128)(2,1)}, bf16[384,768]{1,0:T(8,128)(2,1)}, u32[]{:S(2)}, u32[]{:S(2)}) collective-permute-start(bf16[384,768]{1,0:T(8,128)(2,1)} %refs_12_.1), channel_id=1, source_target_pairs={{0,4},{1,5},{2,6},{3,7},{4,0},{5,1},{6,2},{7,3},{8,12},{9,13},{10,... | collective-permute-start | bytes 1769480 | tf_op jit(solution)/shard_map/ppermute | solution.py:675
  38.0 32.9 %collective-permute-start.15 = (bf16[384,768]{1,0:T(8,128)(2,1)}, bf16[384,768]{1,0:T(8,128)(2,1)}, u32[]{:S(2)}, u32[]{:S(2)}) collective-permute-start(bf16[384,768]{1,0:T(8,128)(2,1)} %refs_12_.1), channel_id=1, source_target_pairs={{0,2},{1,3},{2,0},{3,1},{4,6},{5,7},{6,4},{7,5},{8,10},{9,11},{10,... | collective-permute-start | bytes 1769480 | tf_op jit(solution)/shard_map/ppermute | solution.py:675
  51.8 19.1 %collective-permute-start.13 = (bf16[48,3072]{1,0:T(8,128)(2,1)S(1)}, bf16[48,3072]{1,0:T(8,128)(2,1)S(1)}, u32[]{:S(2)}, u32[]{:S(2)}) collective-permute-start(bf16[48,3072]{1,0:T(8,128)(2,1)S(1)} %slice.249), channel_id=1, source_target_pairs={{0,2},{1,3},{2,0},{3,1},{4,6},{5,7},{6,4},{7,5},{8,10},{9,11},{10,... | collective-permute-start | bytes 884744 | tf_op jit(solution)/shard_map/ppermute | solution.py:675
  52.3 18.7 %collective-permute-start.14 = (bf16[48,3072]{1,0:T(8,128)(2,1)S(1)}, bf16[48,3072]{1,0:T(8,128)(2,1)S(1)}, u32[]{:S(2)}, u32[]{:S(2)}) collective-permute-start(bf16[48,3072]{1,0:T(8,128)(2,1)S(1)} %slice.250), channel_id=1, source_target_pairs={{0,4},{1,5},{2,6},{3,7},{4,0},{5,1},{6,2},{7,3},{8,12},{9,13},{10,... | collective-permute-start | bytes 884744 | tf_op jit(solution)/shard_map/ppermute | solution.py:675
  75.4 9.7 %collective-permute-start.22 = (bf16[192,768]{1,0:T(8,128)(2,1)}, bf16[192,768]{1,0:T(8,128)(2,1)S(1)}, u32[]{:S(2)}, u32[]{:S(2)}) collective-permute-start(bf16[192,768]{1,0:T(8,128)(2,1)} %slice.252), channel_id=1, source_target_pairs={{0,4},{1,5},{2,6},{3,7},{4,0},{5,1},{6,2},{7,3},{8,12},{9,13},{10,... | collective-permute-start | bytes 884744 | tf_op jit(solution)/shard_map/ppermute | solution.py:675
  107.2 32.9 %collective-permute-start.28 = (bf16[4,384,768]{2,1,0:T(8,128)(2,1)}, bf16[4,384,768]{2,1,0:T(8,128)(2,1)}, u32[]{:S(2)}, u32[]{:S(2)}) collective-permute-start(bf16[4,384,768]{2,1,0:T(8,128)(2,1)} %get-tuple-element.135), channel_id=1, source_target_pairs={{0,1},{1,0},{2,3},{3,2},{4,5},{5,4},{6,7},{7,6},{8,9},{9,8},{10,11... | collective-permute-start | bytes 7077896 | tf_op jit(solution)/shard_map/ppermute | solution.py:675
  107.4 38.3 %collective-permute-start.29 = (bf16[4,384,768]{2,1,0:T(8,128)(2,1)}, bf16[4,384,768]{2,1,0:T(8,128)(2,1)}, u32[]{:S(2)}, u32[]{:S(2)}) collective-permute-start(bf16[4,384,768]{2,1,0:T(8,128)(2,1)} %get-tuple-element.140), channel_id=1, source_target_pairs={{0,1},{1,0},{2,3},{3,2},{4,5},{5,4},{6,7},{7,6},{8,9},{9,8},{10,11... | collective-permute-start | bytes 7077896 | tf_op jit(solution)/shard_map/ppermute | solution.py:675
  142.8 25.4 %collective-permute-start.33 = (bf16[2,192,768]{2,1,0:T(8,128)(2,1)}, bf16[2,192,768]{2,1,0:T(8,128)(2,1)}, u32[]{:S(2)}, u32[]{:S(2)}) collective-permute-start(bf16[2,192,768]{2,1,0:T(8,128)(2,1)} %get-tuple-element.185), channel_id=1, source_target_pairs={{0,4},{1,5},{2,6},{3,7},{4,0},{5,1},{6,2},{7,3},{8,12},{9,13},{10,... | collective-permute-start | bytes 1769480 | tf_op jit(solution)/shard_map/ppermute | solution.py:675
  144.4 23.9 %collective-permute-start.32 = (bf16[2,192,768]{2,1,0:T(8,128)(2,1)}, bf16[2,192,768]{2,1,0:T(8,128)(2,1)}, u32[]{:S(2)}, u32[]{:S(2)}) collective-permute-start(bf16[2,192,768]{2,1,0:T(8,128)(2,1)} %get-tuple-element.186), channel_id=1, source_target_pairs={{0,2},{1,3},{2,0},{3,1},{4,6},{5,7},{6,4},{7,5},{8,10},{9,11},{10,... | collective-permute-start | bytes 1769480 | tf_op jit(solution)/shard_map/ppermute | solution.py:675
  151.7 20.9 %collective-permute-start.31 = (bf16[2,48,3200]{2,1,0:T(8,128)(2,1)}, bf16[2,48,3200]{2,1,0:T(8,128)(2,1)}, u32[]{:S(2)}, u32[]{:S(2)}) collective-permute-start(bf16[2,48,3200]{2,1,0:T(8,128)(2,1)} %get-tuple-element.179), channel_id=1, source_target_pairs={{0,4},{1,5},{2,6},{3,7},{4,0},{5,1},{6,2},{7,3},{8,12},{9,13},{10,... | collective-permute-start | bytes 1843208 | tf_op jit(solution)/shard_map/ppermute | solution.py:675
  152.2 21.8 %collective-permute-start.30 = (bf16[2,48,3200]{2,1,0:T(8,128)(2,1)}, bf16[2,48,3200]{2,1,0:T(8,128)(2,1)}, u32[]{:S(2)}, u32[]{:S(2)}) collective-permute-start(bf16[2,48,3200]{2,1,0:T(8,128)(2,1)} %get-tuple-element.180), channel_id=1, source_target_pairs={{0,2},{1,3},{2,0},{3,1},{4,6},{5,7},{6,4},{7,5},{8,10},{9,11},{10,... | collective-permute-start | bytes 1843208 | tf_op jit(solution)/shard_map/ppermute | solution.py:675
  153.0 30.4 %collective-permute-start.38 = (bf16[4,192,768]{2,1,0:T(8,128)(2,1)}, bf16[4,192,768]{2,1,0:T(8,128)(2,1)}, u32[]{:S(2)}, u32[]{:S(2)}) collective-permute-start(bf16[4,192,768]{2,1,0:T(8,128)(2,1)} %get-tuple-element.182), channel_id=1, source_target_pairs={{0,8},{8,0},{16,24},{24,16},{1,9},{9,1},{17,25},{25,17},{2,10},{10... | collective-permute-start | bytes 3538952 | tf_op jit(solution)/shard_map/ppermute | solution.py:728
  169.9 10.4 %collective-permute-start.37 = (bf16[192,768]{1,0:T(8,128)(2,1)S(1)}, bf16[192,768]{1,0:T(8,128)(2,1)S(1)}, u32[]{:S(2)}, u32[]{:S(2)}) collective-permute-start(bf16[192,768]{1,0:T(8,128)(2,1)S(1)} %get-tuple-element.183), channel_id=1, source_target_pairs={{0,2},{1,3},{2,0},{3,1},{4,6},{5,7},{6,4},{7,5},{8,10},{9,11},{10,... | collective-permute-start | bytes 884744 | tf_op jit(solution)/shard_map/ppermute | solution.py:675
  175.5 11.2 %collective-permute-start.35 = (bf16[48,3200]{1,0:T(8,128)(2,1)S(1)}, bf16[48,3200]{1,0:T(8,128)(2,1)S(1)}, u32[]{:S(2)}, u32[]{:S(2)}) collective-permute-start(bf16[48,3200]{1,0:T(8,128)(2,1)S(1)} %get-tuple-element.177), channel_id=1, source_target_pairs={{0,2},{1,3},{2,0},{3,1},{4,6},{5,7},{6,4},{7,5},{8,10},{9,11},{10,... | collective-permute-start | bytes 921608 | tf_op jit(solution)/shard_map/ppermute | solution.py:675
  176.8 9.9 %collective-permute-start.34 = (bf16[48,3200]{1,0:T(8,128)(2,1)S(1)}, bf16[48,3200]{1,0:T(8,128)(2,1)S(1)}, u32[]{:S(2)}, u32[]{:S(2)}) collective-permute-start(bf16[48,3200]{1,0:T(8,128)(2,1)S(1)} %get-tuple-element.178), channel_id=1, source_target_pairs={{0,4},{1,5},{2,6},{3,7},{4,0},{5,1},{6,2},{7,3},{8,12},{9,13},{10,... | collective-permute-start | bytes 921608 | tf_op jit(solution)/shard_map/ppermute | solution.py:675
  184.6 10.6 %collective-permute-start.42 = (bf16[2,96,768]{2,1,0:T(8,128)(2,1)S(1)}, bf16[2,96,768]{2,1,0:T(8,128)(2,1)S(1)}, u32[]{:S(2)}, u32[]{:S(2)}) collective-permute-start(bf16[2,96,768]{2,1,0:T(8,128)(2,1)S(1)} %get-tuple-element.191), channel_id=1, source_target_pairs={{0,4},{1,5},{2,6},{3,7},{4,0},{5,1},{6,2},{7,3},{8,12},{9,13},{10,... | collective-permute-start | bytes 884744 | tf_op jit(solution)/shard_map/ppermute | solution.py:675
  185.6 9.6 %collective-permute-start.41 = (bf16[2,96,768]{2,1,0:T(8,128)(2,1)S(1)}, bf16[2,96,768]{2,1,0:T(8,128)(2,1)S(1)}, u32[]{:S(2)}, u32[]{:S(2)}) collective-permute-start(bf16[2,96,768]{2,1,0:T(8,128)(2,1)S(1)} %get-tuple-element.192), channel_id=1, source_target_pairs={{0,2},{1,3},{2,0},{3,1},{4,6},{5,7},{6,4},{7,5},{8,10},{9,11},{10,... | collective-permute-start | bytes 884744 | tf_op jit(solution)/shard_map/ppermute | solution.py:675
  188.6 21.2 %collective-permute-start.39 = (bf16[48,3200]{1,0:T(8,128)(2,1)S(1)}, bf16[48,3200]{1,0:T(8,128)(2,1)}, u32[]{:S(2)}, u32[]{:S(2)}) collective-permute-start(bf16[48,3200]{1,0:T(8,128)(2,1)S(1)} %select_convert_fusion.2), channel_id=1, source_target_pairs={{0,8},{8,0},{16,24},{24,16},{1,9},{9,1},{17,25},{25,17},{2,10},{10... | collective-permute-start | bytes 921608 | tf_op jit(solution)/shard_map/ppermute | solution.py:754
  192.6 19.0 %collective-permute-start.43 = (bf16[192,768]{1,0:T(8,128)(2,1)}, bf16[192,768]{1,0:T(8,128)(2,1)}, u32[]{:S(2)}, u32[]{:S(2)}) collective-permute-start(bf16[192,768]{1,0:T(8,128)(2,1)} %add_convert_fusion.10), channel_id=1, source_target_pairs={{0,24},{24,0},{8,16},{16,8},{1,25},{25,1},{9,17},{17,9},{2,26},{26... | collective-permute-start | bytes 884744 | tf_op jit(solution)/shard_map/ppermute | solution.py:764
  197.9 29.9 %collective-permute-start.46 = (bf16[96,768]{1,0:T(8,128)(2,1)}, bf16[96,768]{1,0:T(8,128)(2,1)S(1)}, u32[]{:S(2)}, u32[]{:S(2)}) collective-permute-start(bf16[96,768]{1,0:T(8,128)(2,1)} %get-tuple-element.189), channel_id=1, source_target_pairs={{0,2},{1,3},{2,0},{3,1},{4,6},{5,7},{6,4},{7,5},{8,10},{9,11},{10,... | collective-permute-start | bytes 442376 | tf_op jit(solution)/shard_map/ppermute | solution.py:675
  199.1 28.7 %collective-permute-start.45 = (bf16[96,768]{1,0:T(8,128)(2,1)}, bf16[96,768]{1,0:T(8,128)(2,1)}, u32[]{:S(2)}, u32[]{:S(2)}) collective-permute-start(bf16[96,768]{1,0:T(8,128)(2,1)} %get-tuple-element.190), channel_id=1, source_target_pairs={{0,4},{1,5},{2,6},{3,7},{4,0},{5,1},{6,2},{7,3},{8,12},{9,13},{10,... | collective-permute-start | bytes 442376 | tf_op jit(solution)/shard_map/ppermute | solution.py:675
  212.8 19.3 %collective-permute-start.50 = (bf16[192,768]{1,0:T(8,128)(2,1)S(1)}, bf16[192,768]{1,0:T(8,128)(2,1)}, u32[]{:S(2)}, u32[]{:S(2)}) collective-permute-start(bf16[192,768]{1,0:T(8,128)(2,1)S(1)} %add_convert_fusion.9), channel_id=1, source_target_pairs={{0,8},{8,0},{16,24},{24,16},{1,9},{9,1},{17,25},{25,17},{2,10},{10... | collective-permute-start | bytes 884744 | tf_op jit(solution)/shard_map/ppermute | solution.py:770
  213.5 19.6 %collective-permute-start.44 = (bf16[48,3200]{1,0:T(8,128)(2,1)S(1)}, bf16[48,3200]{1,0:T(8,128)(2,1)S(1)}, u32[]{:S(2)}, u32[]{:S(2)}) collective-permute-start(bf16[48,3200]{1,0:T(8,128)(2,1)S(1)} %add_convert_fusion.5), channel_id=1, source_target_pairs={{0,24},{24,0},{8,16},{16,8},{1,25},{25,1},{9,17},{17,9},{2,26},{26... | collective-permute-start | bytes 921608 | tf_op jit(solution)/shard_map/ppermute | solution.py:764
  229.1 11.1 %collective-permute-start.48 = (bf16[192,768]{1,0:T(8,128)(2,1)S(1)}, bf16[192,768]{1,0:T(8,128)(2,1)S(1)}, u32[]{:S(2)}, u32[]{:S(2)}) collective-permute-start(bf16[192,768]{1,0:T(8,128)(2,1)S(1)} %pad_maximum_fusion.1), channel_id=1, source_target_pairs={{0,24},{24,0},{8,16},{16,8},{1,25},{25,1},{9,17},{17,9},{2,26},{26... | collective-permute-start | bytes 884744 | tf_op jit(solution)/shard_map/ppermute | solution.py:764
  233.2 12.3 %collective-permute-start.47 = (bf16[48,3200]{1,0:T(8,128)(2,1)S(1)}, bf16[48,3200]{1,0:T(8,128)(2,1)S(1)}, u32[]{:S(2)}, u32[]{:S(2)}) collective-permute-start(bf16[48,3200]{1,0:T(8,128)(2,1)S(1)} %add_convert_fusion.4), channel_id=1, source_target_pairs={{0,8},{8,0},{16,24},{24,16},{1,9},{9,1},{17,25},{25,17},{2,10},{10... | collective-permute-start | bytes 921608 | tf_op jit(solution)/shard_map/ppermute | solution.py:770
  240.2 9.4 %collective-permute-start.49 = (bf16[192,768]{1,0:T(8,128)(2,1)S(1)}, bf16[192,768]{1,0:T(8,128)(2,1)S(1)}, u32[]{:S(2)}, u32[]{:S(2)}) collective-permute-start(bf16[192,768]{1,0:T(8,128)(2,1)S(1)} %add_convert_fusion.8), channel_id=1, source_target_pairs={{0,8},{8,0},{16,24},{24,16},{1,9},{9,1},{17,25},{25,17},{2,10},{10... | collective-permute-start | bytes 884744 | tf_op jit(solution)/shard_map/ppermute | solution.py:770
  (61 other events, 506.1 us)
where the time goes:
time: 256 us; the launch traced here: 251 us
  Pallas kernels  119 us (46%)
  starting transfers between devices  45.1 us (18%)
  waiting for transfers between devices  38.2 us (15%)
  other arithmetic  33 us (13%)
  local copies, waits for them, and re-layouts  13.2 us (5%)
    pallas_call x1, Pallas kernels, local(): pl.pallas_call(functools.partial(attend_back_kernel, attn_count, seq, row...  32.2 us
    ppermute x42, starting transfers between devices, swap(): return lax.ppermute(value, 'shard', [(i, i ^ bit) for i in range(8)])  31.1 us
    ppermute x42, waiting for transfers between devices, swap(): return lax.ppermute(value, 'shard', [(i, i ^ bit) for i in range(8)])  28.3 us
    pallas_call x2, Pallas kernels, ffn(): pl.pallas_call(functools.partial(ffn_kernel, (inner_count, back_count)),...  27 us
    pallas_call x1, Pallas kernels, local(): pl.pallas_call(functools.partial(attend_kernel, attn_count, seq), grid=gr...  17 us
    pallas_call x1, Pallas kernels, local(): pl.pallas_call(functools.partial(ffn_back_kernel, (inner_count, back_coun...  16.9 us
    pallas_call x1, Pallas kernels, local(): pl.pallas_call(functools.partial(input_grad_kernel, attn_count, seq), gri...  10 us
    pallas_call x1, Pallas kernels, local(): pl.pallas_call(functools.partial(project_kernel, attn_count, rows), grid=...  9.79 us
  transfers between devices with their start and end apart: 51, of which 12 were waited for; matrix products, arithmetic and copies ran while one was open for 15% of the time, Pallas kernels for 41%

commit v1 on v0

--- a/solution.py
+++ b/solution.py
@@ -129,20 +129,9 @@
         qkv[:, columns] = value.astype(BF16)
 
 
-def attend_kernel(count, seq, *refs):
-    offsets, base, words, regions = refs[:4]
-    pieces = refs[4 : 4 + count]
-    tokens, cotangent, qkv, pos, vectors, hidden, compact, proj, mixed, sems = refs[4 + count :]
-    width = tokens.shape[1]
+def attend_kernel(seq, words, regions, qkv, mixed):
+    width = mixed.shape[1]
     step = pl.program_id(0)
-
-    @pl.when(step == 0)
-    def _():
-        copies = start_pieces(pieces, offsets, proj, sems, 3 * width)
-        compact[...] = jnp.zeros_like(compact)
-        for copy in copies:
-            copy.wait()
-
     for k in range(STEP // seq):
         rows = slice(k * seq, (k + 1) * seq)
         pair = step * (STEP // seq) + k
@@ -156,6 +145,22 @@
             expo = jnp.exp(scores - jnp.max(scores, -1, keepdims=True)).astype(BF16)
             both = mm(expo, jnp.concatenate([values, jnp.ones_like(values)], 1))
             mixed[rows, lanes] = (unstacked(both[:, :128]) / unstacked(both[:, 128:])).astype(BF16)
+
+
+def settle_kernel(count, seq, *refs):
+    offsets, base = refs[:2]
+    pieces = refs[2 : 2 + count]
+    tokens, cotangent, mixed, pos, vectors, hidden, compact, proj, sems = refs[2 + count :]
+    width = tokens.shape[1]
+    step = pl.program_id(0)
+
+    @pl.when(step == 0)
+    def _():
+        copies = start_pieces(pieces, offsets, proj, sems, 3 * width)
+        compact[...] = jnp.zeros_like(compact)
+        for copy in copies:
+            copy.wait()
+
     branch = mm(mixed[...], proj[...]) + vectors[2:3, :]
     normed, scale = norm_parts(tokens[...].astype(F32) + branch)
     value = normed * vectors[3:4, :] + vectors[4:5, :]
@@ -689,6 +694,11 @@
     half = mine.shape[0] // 2
     near = [(mine, 0, 0), (by_x, XBIT, 0), (by_y, YBIT, 0)]
     return near + [(by_both[0], far, 0), (by_both[1], far, half)]
+
+
+def chip_pieces(mine, others):
+    keys = (0, XBIT, YBIT, XBIT | YBIT)
+    return [(v, key, 0) for v, key in zip((mine,) + tuple(others), keys)]
 
 
 def with_core(pieces, others):
@@ -863,18 +873,20 @@
     )
     vectors = jnp.pad(vectors, ((0, 0), (0, 128 - vectors.shape[1])))
     attn_shard = jnp.concatenate([qkv_weight, out_weight, vectors], 1)
-    def offsets(size):
+    def offsets(size, halves):
         if not cube:
             return jnp.zeros((1,), jnp.int32)
-        keys = jnp.array([0, XBIT, YBIT, XBIT | YBIT, XBIT | YBIT], jnp.int32)
-        starts = jnp.array([0, 0, 0, 0, size // 2], jnp.int32)
-        return jnp.concatenate([(keys ^ me) * size + starts, (keys ^ me ^ CORE) * size + starts])
-
-    small_offsets, back_offsets = offsets(rows), offsets(back_weight.shape[0])
+        keys = [0, XBIT, YBIT, XBIT | YBIT] + [XBIT | YBIT] * halves
+        keys = jnp.array(keys, jnp.int32) ^ me
+        starts = jnp.array([0] * 4 + [size // 2] * halves, jnp.int32)
+        return jnp.concatenate([keys * size + starts, (keys ^ CORE) * size + starts])
+
+    attn_offsets, inner_offsets = offsets(rows, 1), offsets(rows, 0)
+    back_offsets = offsets(back_weight.shape[0], 0)
     order = jnp.arange(BLOCKS, dtype=jnp.int32)
     if cube:
         order = jnp.array([0, 2, 6, 4, 1, 3, 7, 5], jnp.int32) ^ me
-    indices = (base, pos, blocks, small_offsets, back_offsets, order)
+    indices = (base, pos, blocks, attn_offsets, inner_offsets, back_offsets, order)
     if cube:
         attn_x, attn_y = swap(attn_shard, XBIT), swap(attn_shard, YBIT)
         own = [swap(v, CORE) for v in (attn_shard, inner_weight, back_weight)]
@@ -893,11 +905,11 @@
             [(lax.all_gather(v, "shard", axis=0, tiled=True), 0, 0)]
             for v in (attn_shard, inner_weight, back_weight)
         )
-    base, pos, blocks, small_offsets, back_offsets, order = indices
+    base, pos, blocks, attn_offsets, inner_offsets, back_offsets, order = indices
 
     columns = 4 * width + 128
     attn_count = len(attn)
-    attn_offsets, attn_pieces = small_offsets, [v for v, _, _ in attn]
+    attn_pieces = [v for v, _, _ in attn]
     qkv, vector_rows, inner_bias_full = pl.pallas_call(
         functools.partial(project_kernel, attn_count, rows),
         grid=grid,
@@ -918,45 +930,50 @@
     )(attn_offsets, *attn_pieces, tokens)
     if cube:
         inner_x, inner_y, qkv = lax.optimization_barrier((inner_x, inner_y, qkv))
-        inner_far = far_swap(inner_x, inner_y)
+        inner_far = swap(inner_y, XBIT)
+        inner_core = swap(inner_x, CORE), swap(inner_y, CORE)
+    mixed = pl.pallas_call(
+        functools.partial(attend_kernel, seq),
+        grid=grid,
+        in_specs=[SCALARS] * 2 + [steps(3 * width)],
+        out_specs=steps(width),
+        out_shape=shape_of(count, width),
+        compiler_params=params(),
+        cost_estimate=cost(8),
+        name="attend",
+    )(word_counts, region_counts, qkv)
+    if cube:
+        back_x, back_y, inner_core, mixed = lax.optimization_barrier(
+            (back_x, back_y, inner_core, mixed)
+        )
+        back_far = swap(back_x, YBIT)
+        back_core = swap(back_x, CORE), swap(back_y, CORE)
     hidden1, compact = pl.pallas_call(
-        functools.partial(attend_kernel, attn_count, seq),
+        functools.partial(settle_kernel, attn_count, seq),
         grid=grid,
-        in_specs=[SCALARS] * 4
+        in_specs=[SCALARS] * 2
         + [ANYWHERE] * attn_count
-        + [steps(width), steps(width), steps(3 * width), whole((pairs, 1, seq)), whole((16, width))],
+        + [steps(width)] * 3
+        + [whole((pairs, 1, seq)), whole((16, width))],
         out_specs=[steps(width), whole((cap, columns))],
         out_shape=[shape_of(count, width, dtype=F32), shape_of(cap, columns)],
         scratch_shapes=[
             pltpu.VMEM((width, width), BF16),
-            pltpu.VMEM((STEP, width), BF16),
             pltpu.SemaphoreType.DMA((attn_count,)),
         ],
         compiler_params=params(),
-        cost_estimate=cost(14),
-        name="attend",
-    )(
-        attn_offsets,
-        base,
-        word_counts,
-        region_counts,
-        *attn_pieces,
-        tokens,
-        cotangent,
-        qkv,
-        pos,
-        vector_rows,
-    )
+        cost_estimate=cost(9),
+        name="settle",
+    )(attn_offsets, base, *attn_pieces, tokens, cotangent, mixed, pos, vector_rows)
 
     if cube:
-        inner_x, inner_y, inner_far, back_x, back_y = lax.optimization_barrier(
-            (inner_x, inner_y, inner_far, back_x, back_y, hidden1)
-        )[:5]
-        back_far = far_swap(back_x, back_y)
-        inner_core = [own[1]] + [swap(v, CORE) for v in (inner_x, inner_y) + inner_far]
-        inner = with_core(near_and_far(inner_weight, inner_x, inner_y, inner_far), inner_core)
+        inner_far, back_far, back_core, hidden1 = lax.optimization_barrier(
+            (inner_far, back_far, back_core, hidden1)
+        )
+        inner = chip_pieces(inner_weight, (inner_x, inner_y, inner_far))
+        inner = with_core(inner, (own[1],) + inner_core + (swap(inner_far, CORE),))
     inner_count = len(inner)
-    inner_offsets, inner_pieces = small_offsets, [v for v, _, _ in inner]
+    inner_pieces = [v for v, _, _ in inner]
     in_vmem = pl.BlockSpec(memory_space=pltpu.VMEM)
     live_act, live_slope = pl.pallas_call(
         functools.partial(live_inner_kernel, inner_count),
@@ -977,9 +994,8 @@
     )(inner_offsets, blocks, *inner_pieces, compact, inner_bias_full)
 
     if cube:
-        back_far, back_near, live_act = lax.optimization_barrier((back_far, (back_x, back_y), live_act))
-        back_core = [own[2]] + [swap(v, CORE) for v in back_near + back_far]
-        back = with_core(near_and_far(back_weight, *back_near, back_far), back_core)
+        back = chip_pieces(back_weight, (back_x, back_y, back_far))
+        back = with_core(back, (own[2],) + back_core + (swap(back_far, CORE),))
     back_count = len(back)
     back_pieces = [v for v, _, _ in back]
 

time: 256 us -> 255 us (level)
  local copies, waits for them, and re-layouts: 13.2 us -> 9.99 us
  Pallas kernels: 119 us -> 122 us
  starting transfers between devices: 45.1 us -> 42.1 us
  waiting for transfers between devices: 38.2 us -> 40.8 us
    slice x6 -> x2, local copies, waits for them, and re-layouts: 3.47 us -> 0.04 us  [far_swap(): return (swap(by_y[:half], XBIT), swap(by_x[half:], YBIT))]
    pallas_call x1 -> x2, Pallas kernels: 17 us -> 19.8 us  [the longest x1 10.2 us: local(): pl.pallas_call(functools.partial(settle_kernel, attn_count, seq), grid=gr...]
    ppermute x42 -> x38, starting transfers between devices: 31.1 us -> 29.3 us  [swap(): return lax.ppermute(value, 'shard', [(i, i ^ bit) for i in range(8)])]
    ppermute x42 -> x38, waiting for transfers between devices: 28.3 us -> 28.8 us  [swap(): return lax.ppermute(value, 'shard', [(i, i ^ bit) for i in range(8)])]
  transfers between devices with their start and end apart: 51 -> 47, of which waited for: 12 -> 15; matrix products, arithmetic and copies ran while one was open for 15% -> 14% of each run, Pallas kernels for 41% -> 42%
where the time goes in v1:
time: 255 us; the launch traced here: 250 us
  Pallas kernels  122 us (48%)
  starting transfers between devices  42.1 us (17%)
  waiting for transfers between devices  40.8 us (16%)
  other arithmetic  33 us (13%)
  local copies, waits for them, and re-layouts  9.99 us (4%)
    pallas_call x1, Pallas kernels, local(): pl.pallas_call(functools.partial(attend_back_kernel, attn_count, seq, row...  32.1 us
    ppermute x38, starting transfers between devices, swap(): return lax.ppermute(value, 'shard', [(i, i ^ bit) for i in range(8)])  29.3 us
    ppermute x38, waiting for transfers between devices, swap(): return lax.ppermute(value, 'shard', [(i, i ^ bit) for i in range(8)])  28.8 us
    pallas_call x2, Pallas kernels, ffn(): pl.pallas_call(functools.partial(ffn_kernel, (inner_count, back_count)),...  26.8 us
    pallas_call x1, Pallas kernels, local(): pl.pallas_call(functools.partial(ffn_back_kernel, (inner_count, back_coun...  16.8 us
    pallas_call x1, Pallas kernels, local(): pl.pallas_call(functools.partial(settle_kernel, attn_count, seq), grid=gr...  10.2 us
    pallas_call x1, Pallas kernels, local(): pl.pallas_call(functools.partial(input_grad_kernel, attn_count, seq), gri...  10 us
    pallas_call x1, Pallas kernels, local(): pl.pallas_call(functools.partial(project_kernel, attn_count, rows), grid=...  9.76 us
  transfers between devices with their start and end apart: 47, of which 15 were waited for; matrix products, arithmetic and copies ran while one was open for 14% of the time, Pallas kernels for 42%

profile of v1, /device:TPU:0, one launch (start us, length us, event | category | flops | bytes accessed | tf_op | source)
XLA Modules:
  0.0 250.1 jit_solution(9634915789273554406)
XLA Ops:
  4.3 2.6 %collective-permute-start.1 = (bf16[96,3200]{1,0:T(8,128)(2,1)S(1)}, bf16[96,3200]{1,0:T(8,128)(2,1)S(1)}, u32[]{:S(2)}, u32[]{:S(2)}) collective-permute-start(bf16[96,3200]{1,0:T(8,128)(2,1)S(1)} %fusion.1.refs_1_.refs_2_.refs_6_), channel_id=1, source_target_pairs={{0,4},{1,5},{2,6},{3,7},{4,0},{5,1},{6,2},{7,3},{8,12},{9,13},{10,... | collective-permute-start | bytes 1843208 | tf_op jit(solution)/shard_map/ppermute | solution.py:680
  13.9 7.4 %collective-permute-done.1.refs_3_.refs_4_.refs_8_ = bf16[96,3200]{1,0:T(8,128)(2,1)S(1)} collective-permute-done((bf16[96,3200]{1,0:T(8,128)(2,1)S(1)}, bf16[96,3200]{1,0:T(8,128)(2,1)S(1)}, u32[]{:S(2)}, u32[]{:S(2)}) %collective-permute-start.1) | collective-permute-done | bytes 614432 | tf_op jit(solution)/shard_map/ppermute | solution.py:680
  27.0 5.6 %collective-permute-done.7.refs_4_.refs_5_.refs_9_ = bf16[48,3200]{1,0:T(8,128)(2,1)S(1)} collective-permute-done((bf16[48,3200]{1,0:T(8,128)(2,1)S(1)}, bf16[48,3200]{1,0:T(8,128)(2,1)S(1)}, u32[]{:S(2)}, u32[]{:S(2)}) %collective-permute-start.7) | collective-permute-done | bytes 307232 | tf_op jit(solution)/shard_map/ppermute | solution.py:680
  39.3 9.8 %project.1 = (bf16[1024,2304]{1,0:T(8,128)(2,1)}, f32[16,768]{1,0:T(8,128)}, f32[1,3072]{1,0:T(1,128)}) custom-call(s32[10]{0:T(128)} %pad_add_fusion.1.refs_0_, bf16[96,3200]{1,0:T(8,128)(2,1)} %copy-done, bf16[96,3200]{1,0:T(8,128)(2,1)} %copy-done.2, bf16[96,3200]{1,0:T(8,128)(2,1)} %copy-done.1, bf16[48,3200]{1,0:T(8,128)(2,1)} %copy-done.15, ...), custom_call_target="tpu_custom_call" | custom-call | flops 900000000 | tf_op jit(solution)/shard_map/project/pallas_call | solution.py:913
  51.2 9.6 %attend.1.refs_14_ = bf16[1024,768]{1,0:T(8,128)(2,1)} custom-call(s32[8]{0:T(128)} %refs_3_.1, s32[8]{0:T(128)} %refs_4_.2, bf16[1024,2304]{1,0:T(8,128)(2,1)} %get-tuple-element.106.qkv.refs_18_), custom_call_target="tpu_custom_call" | custom-call | flops 800000000 | tf_op jit(solution)/shard_map/attend/pallas_call | solution.py:935
  62.8 10.2 %settle.1 = (f32[1024,768]{1,0:T(8,128)}, bf16[768,3200]{1,0:T(8,128)(2,1)}) custom-call(s32[10]{0:T(128)} %pad_add_fusion.1.refs_0_, s32[9]{0:T(128)} %copy-done.28, bf16[96,3200]{1,0:T(8,128)(2,1)} %copy-done, bf16[96,3200]{1,0:T(8,128)(2,1)} %copy-done.2, bf16[96,3200]{1,0:T(8,128)(2,1)} %copy-done.1, bf16[48,3200]{1,0:T(8,128)(2,1)} %copy-done.15, ...), custom_call_target="tpu_custom_call" | custom-call | flops 900000000 | tf_op jit(solution)/shard_map/settle/pallas_call | solution.py:951
  73.1 4.8 %collective-permute-done.18.refs_15_.refs_13_ = bf16[384,768]{1,0:T(8,128)(2,1)S(1)} collective-permute-done((bf16[384,768]{1,0:T(8,128)(2,1)}, bf16[384,768]{1,0:T(8,128)(2,1)S(1)}, u32[]{:S(2)}, u32[]{:S(2)}) %collective-permute-start.18) | collective-permute-done | bytes 589856 | tf_op jit(solution)/shard_map/ppermute | solution.py:680
  80.7 6.6 %live_inner.1 = (bf16[768,3072]{1,0:T(8,128)(2,1)}, bf16[768,3072]{1,0:T(8,128)(2,1)}) custom-call(s32[8]{0:T(128)} %pad_add_fusion.2.refs_0_, s32[1]{0:T(128)S(6)} %max.3.refs_1_.refs_3_.refs_5_, bf16[96,3072]{1,0:T(8,128)(2,1)} %refs_2_.2, bf16[96,3072]{1,0:T(8,128)(2,1)} %collective-permute-done.5.refs_3_.refs_5_, ...), custom_call_target="tpu_custom_call" | custom-call | flops 600000000 | tf_op jit(solution)/shard_map/live_inner/pallas_call | solution.py:978
  88.2 16.8 %ffn_back.1 = (bf16[4,384,768]{2,1,0:T(8,128)(2,1)}, bf16[4,384,768]{2,1,0:T(8,128)(2,1)}, bf16[4,384,768]{2,1,0:T(8,128)(2,1)}, bf16[4,384,768]{2,1,0:T(8,128)(...) custom-call(s32[8]{0:T(128)} %pad_add_fusion.2.refs_0_, s32[8]{0:T(128)} %pad_add_fusion.3.refs_1_, ...), custom_call_target="tpu_custom_call" | custom-call | flops 1300000000 | tf_op jit(solution)/shard_map/ffn_back/pallas_call | solution.py:1005
  105.6 32.1 %attend_back.1 = (bf16[1024,2304]{1,0:T(8,128)(2,1)}, bf16[768,768]{1,0:T(8,128)(2,1)}, bf16[4,96,3200]{2,1,0:T(8,128)(2,1)}, bf16[4,96,3200]{2,1,0:T(8,128)(2,1)}) custom-call(s32[10]{0:T(128)} %pad_add_fusion.1.refs_0_, s32[8]{0:T(128)} %broadcast_xor_fusion.refs_2_.refs_1_, s32[9]{0:T(128)} %copy-done.28, s32[8]{0:T(128)} %refs_3_.1, s32[8]{0:T(128)} %refs_4_.2, ...), custom_call_target="tpu_custom_call" | custom-call | flops 2200000000 | tf_op jit(solution)/shard_map/attend_back/pallas_call | solution.py:1057
  137.9 2.7 %add_convert_fusion.2 = (bf16[2,192,768]{2,1,0:T(8,128)(2,1)}, bf16[2,192,768]{2,1,0:T(8,128)(2,1)}) fusion(bf16[4,384,768]{2,1,0:T(8,128)(2,1)} %collective-permute-done.24, bf16[4,384,768]{2,1,0:T(8,128)(2,1)S(1)} %copy-done.19), kind=kLoop, calls=%fused_computation.9 | loop fusion | flops 2359296 | bytes 3538944 | tf_op jit(solution)/shard_map/convert_element_type | solution.py:743
  141.1 3.6 %collective-permute-start.28 = (bf16[2,192,768]{2,1,0:T(8,128)(2,1)}, bf16[2,192,768]{2,1,0:T(8,128)(2,1)}, u32[]{:S(2)}, u32[]{:S(2)}) collective-permute-start(bf16[2,192,768]{2,1,0:T(8,128)(2,1)} %get-tuple-element.186), channel_id=1, source_target_pairs={{0,2},{1,3},{2,0},{3,1},{4,6},{5,7},{6,4},{7,5},{8,10},{9,11},{10,... | collective-permute-start | bytes 1769480 | tf_op jit(solution)/shard_map/ppermute | solution.py:680
  144.7 3.5 %select_convert_fusion = (bf16[4,192,768]{2,1,0:T(8,128)(2,1)S(1)}, bf16[4,192,768]{2,1,0:T(8,128)(2,1)}) fusion(pred[]{:T(512)S(6)} %or.13, bf16[4,384,768]{2,1,0:T(8,128)(2,1)} %collective-permute-done.25, bf16[4,384,768]{2,1,0:T(8,128)(2,1)S(1)} %copy-done.21), kind=kLoop, calls=%fused_computation | loop fusion | flops 5898240 | bytes 7077889 | tf_op jit(solution)/shard_map/convert_element_type | solution.py:737
  148.2 2.6 %add_convert_fusion = (bf16[2,48,3200]{2,1,0:T(8,128)(2,1)}, bf16[2,48,3200]{2,1,0:T(8,128)(2,1)}) fusion(bf16[4,96,3200]{2,1,0:T(8,128)(2,1)} %collective-permute-done.23, bf16[4,96,3200]{2,1,0:T(8,128)(2,1)S(1)} %copy-done.18), kind=kLoop, calls=%fused_computation.5 | loop fusion | flops 2457600 | bytes 3686400 | tf_op jit(solution)/shard_map/convert_element_type | solution.py:743
  150.8 1.6 collective-permute-start.34
  152.4 13.5 %ffn.2.refs_21_ = bf16[1024,768]{1,0:T(8,128)(2,1)} custom-call(s32[8]{0:T(128)} %pad_add_fusion.2.refs_0_, s32[8]{0:T(128)} %pad_add_fusion.3.refs_1_, bf16[96,3072]{1,0:T(8,128)(2,1)} %refs_2_.2, bf16[96,3072]{1,0:T(8,128)(2,1)} %collective-permute-done.5.refs_3_.refs_5_, bf16[96,3072]{1,0:T(8,128)(2,1)} %collective-permute-done.6.refs_4_.refs_6_, ...), custom_call_target="tpu_custom_call" | custom-call | flops 1100000000 | tf_op jit(solution)/shard_map/ffn/pallas_call | solution.py:1115
  165.9 1.6 fusion.5
  170.0 2.2 collective-permute-done.26
  173.7 2.1 collective-permute-start.31
  175.8 2.6 %collective-permute-done.33 = bf16[192,768]{1,0:T(8,128)(2,1)S(1)} collective-permute-done((bf16[192,768]{1,0:T(8,128)(2,1)S(1)}, bf16[192,768]{1,0:T(8,128)(2,1)S(1)}, u32[]{:S(2)}, u32[]{:S(2)}) %collective-permute-start.33) | collective-permute-done | bytes 294944 | tf_op jit(solution)/shard_map/ppermute | solution.py:680
  182.6 2.1 collective-permute-start.38
  185.8 1.7 select_convert_fusion.2
  188.3 2.3 add_convert_fusion.10
  190.6 2.7 %collective-permute-start.39 = (bf16[192,768]{1,0:T(8,128)(2,1)}, bf16[192,768]{1,0:T(8,128)(2,1)}, u32[]{:S(2)}, u32[]{:S(2)}) collective-permute-start(bf16[192,768]{1,0:T(8,128)(2,1)} %add_convert_fusion.10), channel_id=1, source_target_pairs={{0,24},{24,0},{8,16},{16,8},{1,25},{25,1},{9,17},{17,9},{2,26},{26... | collective-permute-start | bytes 884744 | tf_op jit(solution)/shard_map/ppermute | solution.py:774
  194.1 1.9 fusion.9
  197.7 10.0 %input_grad.1 = f32[1024,768]{1,0:T(8,128)} custom-call(s32[10]{0:T(128)} %pad_add_fusion.1.refs_0_, s32[9]{0:T(128)} %copy-done.28, bf16[96,3200]{1,0:T(8,128)(2,1)} %copy-done, bf16[96,3200]{1,0:T(8,128)(2,1)} %copy-done.2, bf16[96,3200]{1,0:T(8,128)(2,1)} %copy-done.1, bf16[48,3200]{1,0:T(8,128)(2,1)} %copy-done.15, bf16[48,3200]{1,0:T(8,128)(2,1)} %copy-done.16, ...), custom_call_target="tpu_custom_call" | custom-call | flops 900000000 | tf_op jit(solution)/shard_map/input_grad/pallas_call | solution.py:1164
  207.7 1.9 add_convert_fusion.5
  212.8 13.3 %ffn.3 = bf16[1024,768]{1,0:T(8,128)(2,1)} custom-call(s32[8]{0:T(128)} %pad_add_fusion.2.refs_0_, s32[8]{0:T(128)} %pad_add_fusion.3.refs_1_, bf16[96,3072]{1,0:T(8,128)(2,1)} %refs_2_.2, bf16[96,3072]{1,0:T(8,128)(2,1)} %collective-permute-done.5.refs_3_.refs_5_, ...), custom_call_target="tpu_custom_call", output_to_operand_aliasing={{}: (21, {})} | custom-call | flops 1100000000 | tf_op jit(solution)/shard_map/ffn/pallas_call | solution.py:1115
  227.4 3.0 %collective-permute-start.44 = (bf16[192,768]{1,0:T(8,128)(2,1)S(1)}, bf16[192,768]{1,0:T(8,128)(2,1)S(1)}, u32[]{:S(2)}, u32[]{:S(2)}) collective-permute-start(bf16[192,768]{1,0:T(8,128)(2,1)S(1)} %pad_maximum_fusion.1), channel_id=1, source_target_pairs={{0,24},{24,0},{8,16},{16,8},{1,25},{25,1},{9,17},{17,9},{2,26},{26... | collective-permute-start | bytes 884744 | tf_op jit(solution)/shard_map/ppermute | solution.py:774
  231.7 7.2 %collective-permute-done.44 = bf16[192,768]{1,0:T(8,128)(2,1)S(1)} collective-permute-done((bf16[192,768]{1,0:T(8,128)(2,1)S(1)}, bf16[192,768]{1,0:T(8,128)(2,1)S(1)}, u32[]{:S(2)}, u32[]{:S(2)}) %collective-permute-start.44) | collective-permute-done | bytes 294944 | tf_op jit(solution)/shard_map/ppermute | solution.py:774
  240.5 2.9 %collective-permute-done.43 = bf16[48,3200]{1,0:T(8,128)(2,1)S(1)} collective-permute-done((bf16[48,3200]{1,0:T(8,128)(2,1)S(1)}, bf16[48,3200]{1,0:T(8,128)(2,1)S(1)}, u32[]{:S(2)}, u32[]{:S(2)}) %collective-permute-start.43) | collective-permute-done | bytes 307232 | tf_op jit(solution)/shard_map/ppermute | solution.py:780
  246.9 1.6 collective-permute-done.45
  (199 shorter events, 55.8 us)
Async XLA Ops:
  4.3 17.0 %collective-permute-start.1 = (bf16[96,3200]{1,0:T(8,128)(2,1)S(1)}, bf16[96,3200]{1,0:T(8,128)(2,1)S(1)}, u32[]{:S(2)}, u32[]{:S(2)}) collective-permute-start(bf16[96,3200]{1,0:T(8,128)(2,1)S(1)} %fusion.1.refs_1_.refs_2_.refs_6_), channel_id=1, source_target_pairs={{0,4},{1,5},{2,6},{3,7},{4,0},{5,1},{6,2},{7,3},{8,12},{9,13},{10,... | collective-permute-start | bytes 1843208 | tf_op jit(solution)/shard_map/ppermute | solution.py:680
  6.9 15.9 %collective-permute-start = (bf16[96,3200]{1,0:T(8,128)(2,1)S(1)}, bf16[96,3200]{1,0:T(8,128)(2,1)S(1)}, u32[]{:S(2)}, u32[]{:S(2)}) collective-permute-start(bf16[96,3200]{1,0:T(8,128)(2,1)S(1)} %fusion.1.refs_1_.refs_2_.refs_6_), channel_id=1, source_target_pairs={{0,2},{1,3},{2,0},{3,1},{4,6},{5,7},{6,4},{7,5},{8,10},{9,11},{10,... | collective-permute-start | bytes 1843208 | tf_op jit(solution)/shard_map/ppermute | solution.py:680
  22.8 12.4 %collective-permute-start.9 = (bf16[96,3200]{1,0:T(8,128)(2,1)S(1)}, bf16[96,3200]{1,0:T(8,128)(2,1)S(1)}, u32[]{:S(2)}, u32[]{:S(2)}) collective-permute-start(bf16[96,3200]{1,0:T(8,128)(2,1)S(1)} %collective-permute-done.refs_2_.refs_3_.refs_7_), channel_id=1, source_target_pairs={{0,1},{1,0},{2,3},{3,2},{4,5},{5,4},{6,7},{7,6},{8,9},{9,8},{10,11... | collective-permute-start | bytes 1843208 | tf_op jit(solution)/shard_map/ppermute | solution.py:680
  22.8 12.4 %collective-permute-start.10 = (bf16[96,3200]{1,0:T(8,128)(2,1)S(1)}, bf16[96,3200]{1,0:T(8,128)(2,1)S(1)}, u32[]{:S(2)}, u32[]{:S(2)}) collective-permute-start(bf16[96,3200]{1,0:T(8,128)(2,1)S(1)} %collective-permute-done.1.refs_3_.refs_4_.refs_8_), channel_id=1, source_target_pairs={{0,1},{1,0},{2,3},{3,2},{4,5},{5,4},{6,7},{7,6},{8,9},{9,8},{10,11... | collective-permute-start | bytes 1843208 | tf_op jit(solution)/shard_map/ppermute | solution.py:680
  25.5 23.6 %collective-permute-start.6 = (bf16[96,3072]{1,0:T(8,128)(2,1)}, bf16[96,3072]{1,0:T(8,128)(2,1)}, u32[]{:S(2)}, u32[]{:S(2)}) collective-permute-start(bf16[96,3072]{1,0:T(8,128)(2,1)} %refs_2_.2), channel_id=1, source_target_pairs={{0,4},{1,5},{2,6},{3,7},{4,0},{5,1},{6,2},{7,3},{8,12},{9,13},{10,... | collective-permute-start | bytes 1769480 | tf_op jit(solution)/shard_map/ppermute | solution.py:680
  32.6 16.6 %collective-permute-start.5 = (bf16[96,3072]{1,0:T(8,128)(2,1)}, bf16[96,3072]{1,0:T(8,128)(2,1)}, u32[]{:S(2)}, u32[]{:S(2)}) collective-permute-start(bf16[96,3072]{1,0:T(8,128)(2,1)} %refs_2_.2), channel_id=1, source_target_pairs={{0,2},{1,3},{2,0},{3,1},{4,6},{5,7},{6,4},{7,5},{8,10},{9,11},{10,... | collective-permute-start | bytes 1769480 | tf_op jit(solution)/shard_map/ppermute | solution.py:680
  36.5 24.3 %collective-permute-start.15 = (bf16[384,768]{1,0:T(8,128)(2,1)}, bf16[384,768]{1,0:T(8,128)(2,1)}, u32[]{:S(2)}, u32[]{:S(2)}) collective-permute-start(bf16[384,768]{1,0:T(8,128)(2,1)} %refs_10_.1), channel_id=1, source_target_pairs={{0,4},{1,5},{2,6},{3,7},{4,0},{5,1},{6,2},{7,3},{8,12},{9,13},{10,... | collective-permute-start | bytes 1769480 | tf_op jit(solution)/shard_map/ppermute | solution.py:680
  38.7 23.0 %collective-permute-start.14 = (bf16[384,768]{1,0:T(8,128)(2,1)}, bf16[384,768]{1,0:T(8,128)(2,1)}, u32[]{:S(2)}, u32[]{:S(2)}) collective-permute-start(bf16[384,768]{1,0:T(8,128)(2,1)} %refs_10_.1), channel_id=1, source_target_pairs={{0,2},{1,3},{2,0},{3,1},{4,6},{5,7},{6,4},{7,5},{8,10},{9,11},{10,... | collective-permute-start | bytes 1769480 | tf_op jit(solution)/shard_map/ppermute | solution.py:680
  49.2 12.6 %collective-permute-start.16 = (bf16[96,3072]{1,0:T(8,128)(2,1)}, bf16[96,3072]{1,0:T(8,128)(2,1)S(1)}, u32[]{:S(2)}, u32[]{:S(2)}) collective-permute-start(bf16[96,3072]{1,0:T(8,128)(2,1)} %collective-permute-done.5.refs_3_.refs_5_), channel_id=1, source_target_pairs={{0,1},{1,0},{2,3},{3,2},{4,5},{5,4},{6,7},{7,6},{8,9},{9,8},{10,11... | collective-permute-start | bytes 1769480 | tf_op jit(solution)/shard_map/ppermute | solution.py:680
  49.2 12.6 %collective-permute-start.17 = (bf16[96,3072]{1,0:T(8,128)(2,1)}, bf16[96,3072]{1,0:T(8,128)(2,1)S(1)}, u32[]{:S(2)}, u32[]{:S(2)}) collective-permute-start(bf16[96,3072]{1,0:T(8,128)(2,1)} %collective-permute-done.6.refs_4_.refs_6_), channel_id=1, source_target_pairs={{0,1},{1,0},{2,3},{3,2},{4,5},{5,4},{6,7},{7,6},{8,9},{9,8},{10,11... | collective-permute-start | bytes 1769480 | tf_op jit(solution)/shard_map/ppermute | solution.py:680
  49.7 23.4 %collective-permute-start.13 = (bf16[96,3072]{1,0:T(8,128)(2,1)}, bf16[96,3072]{1,0:T(8,128)(2,1)S(1)}, u32[]{:S(2)}, u32[]{:S(2)}) collective-permute-start(bf16[96,3072]{1,0:T(8,128)(2,1)} %collective-permute-done.6.refs_4_.refs_6_), channel_id=1, source_target_pairs={{0,2},{1,3},{2,0},{3,1},{4,6},{5,7},{6,4},{7,5},{8,10},{9,11},{10,... | collective-permute-start | bytes 1769480 | tf_op jit(solution)/shard_map/ppermute | solution.py:680
  61.8 11.3 %collective-permute-start.20 = (bf16[384,768]{1,0:T(8,128)(2,1)}, bf16[384,768]{1,0:T(8,128)(2,1)S(1)}, u32[]{:S(2)}, u32[]{:S(2)}) collective-permute-start(bf16[384,768]{1,0:T(8,128)(2,1)} %collective-permute-done.15.refs_14_.refs_12_), channel_id=1, source_target_pairs={{0,1},{1,0},{2,3},{3,2},{4,5},{5,4},{6,7},{7,6},{8,9},{9,8},{10,11... | collective-permute-start | bytes 1769480 | tf_op jit(solution)/shard_map/ppermute | solution.py:680
  61.9 11.2 %collective-permute-start.19 = (bf16[384,768]{1,0:T(8,128)(2,1)}, bf16[384,768]{1,0:T(8,128)(2,1)S(1)}, u32[]{:S(2)}, u32[]{:S(2)}) collective-permute-start(bf16[384,768]{1,0:T(8,128)(2,1)} %collective-permute-done.14.refs_13_.refs_11_), channel_id=1, source_target_pairs={{0,1},{1,0},{2,3},{3,2},{4,5},{5,4},{6,7},{7,6},{8,9},{9,8},{10,11... | collective-permute-start | bytes 1769480 | tf_op jit(solution)/shard_map/ppermute | solution.py:680
  62.4 15.5 %collective-permute-start.18 = (bf16[384,768]{1,0:T(8,128)(2,1)}, bf16[384,768]{1,0:T(8,128)(2,1)S(1)}, u32[]{:S(2)}, u32[]{:S(2)}) collective-permute-start(bf16[384,768]{1,0:T(8,128)(2,1)} %collective-permute-done.14.refs_13_.refs_11_), channel_id=1, source_target_pairs={{0,4},{1,5},{2,6},{3,7},{4,0},{5,1},{6,2},{7,3},{8,12},{9,13},{10,... | collective-permute-start | bytes 1769480 | tf_op jit(solution)/shard_map/ppermute | solution.py:680
  105.0 32.9 %collective-permute-start.24 = (bf16[4,384,768]{2,1,0:T(8,128)(2,1)}, bf16[4,384,768]{2,1,0:T(8,128)(2,1)}, u32[]{:S(2)}, u32[]{:S(2)}) collective-permute-start(bf16[4,384,768]{2,1,0:T(8,128)(2,1)} %get-tuple-element.135), channel_id=1, source_target_pairs={{0,1},{1,0},{2,3},{3,2},{4,5},{5,4},{6,7},{7,6},{8,9},{9,8},{10,11... | collective-permute-start | bytes 7077896 | tf_op jit(solution)/shard_map/ppermute | solution.py:680
  105.2 39.5 %collective-permute-start.25 = (bf16[4,384,768]{2,1,0:T(8,128)(2,1)}, bf16[4,384,768]{2,1,0:T(8,128)(2,1)}, u32[]{:S(2)}, u32[]{:S(2)}) collective-permute-start(bf16[4,384,768]{2,1,0:T(8,128)(2,1)} %get-tuple-element.140), channel_id=1, source_target_pairs={{0,1},{1,0},{2,3},{3,2},{4,5},{5,4},{6,7},{7,6},{8,9},{9,8},{10,11... | collective-permute-start | bytes 7077896 | tf_op jit(solution)/shard_map/ppermute | solution.py:680
  140.6 25.3 %collective-permute-start.29 = (bf16[2,192,768]{2,1,0:T(8,128)(2,1)}, bf16[2,192,768]{2,1,0:T(8,128)(2,1)}, u32[]{:S(2)}, u32[]{:S(2)}) collective-permute-start(bf16[2,192,768]{2,1,0:T(8,128)(2,1)} %get-tuple-element.185), channel_id=1, source_target_pairs={{0,4},{1,5},{2,6},{3,7},{4,0},{5,1},{6,2},{7,3},{8,12},{9,13},{10,... | collective-permute-start | bytes 1769480 | tf_op jit(solution)/shard_map/ppermute | solution.py:680
  141.1 24.8 %collective-permute-start.28 = (bf16[2,192,768]{2,1,0:T(8,128)(2,1)}, bf16[2,192,768]{2,1,0:T(8,128)(2,1)}, u32[]{:S(2)}, u32[]{:S(2)}) collective-permute-start(bf16[2,192,768]{2,1,0:T(8,128)(2,1)} %get-tuple-element.186), channel_id=1, source_target_pairs={{0,2},{1,3},{2,0},{3,1},{4,6},{5,7},{6,4},{7,5},{8,10},{9,11},{10,... | collective-permute-start | bytes 1769480 | tf_op jit(solution)/shard_map/ppermute | solution.py:680
  150.8 19.3 %collective-permute-start.27 = (bf16[2,48,3200]{2,1,0:T(8,128)(2,1)}, bf16[2,48,3200]{2,1,0:T(8,128)(2,1)}, u32[]{:S(2)}, u32[]{:S(2)}) collective-permute-start(bf16[2,48,3200]{2,1,0:T(8,128)(2,1)} %get-tuple-element.179), channel_id=1, source_target_pairs={{0,4},{1,5},{2,6},{3,7},{4,0},{5,1},{6,2},{7,3},{8,12},{9,13},{10,... | collective-permute-start | bytes 1843208 | tf_op jit(solution)/shard_map/ppermute | solution.py:680
  150.8 21.5 %collective-permute-start.26 = (bf16[2,48,3200]{2,1,0:T(8,128)(2,1)}, bf16[2,48,3200]{2,1,0:T(8,128)(2,1)}, u32[]{:S(2)}, u32[]{:S(2)}) collective-permute-start(bf16[2,48,3200]{2,1,0:T(8,128)(2,1)} %get-tuple-element.180), channel_id=1, source_target_pairs={{0,2},{1,3},{2,0},{3,1},{4,6},{5,7},{6,4},{7,5},{8,10},{9,11},{10,... | collective-permute-start | bytes 1843208 | tf_op jit(solution)/shard_map/ppermute | solution.py:680
  150.8 30.6 %collective-permute-start.34 = (bf16[4,192,768]{2,1,0:T(8,128)(2,1)}, bf16[4,192,768]{2,1,0:T(8,128)(2,1)}, u32[]{:S(2)}, u32[]{:S(2)}) collective-permute-start(bf16[4,192,768]{2,1,0:T(8,128)(2,1)} %get-tuple-element.182), channel_id=1, source_target_pairs={{0,8},{8,0},{16,24},{24,16},{1,9},{9,1},{17,25},{25,17},{2,10},{10... | collective-permute-start | bytes 3538952 | tf_op jit(solution)/shard_map/ppermute | solution.py:738
  167.5 10.9 %collective-permute-start.33 = (bf16[192,768]{1,0:T(8,128)(2,1)S(1)}, bf16[192,768]{1,0:T(8,128)(2,1)S(1)}, u32[]{:S(2)}, u32[]{:S(2)}) collective-permute-start(bf16[192,768]{1,0:T(8,128)(2,1)S(1)} %get-tuple-element.183), channel_id=1, source_target_pairs={{0,2},{1,3},{2,0},{3,1},{4,6},{5,7},{6,4},{7,5},{8,10},{9,11},{10,... | collective-permute-start | bytes 884744 | tf_op jit(solution)/shard_map/ppermute | solution.py:680
  173.7 11.3 %collective-permute-start.31 = (bf16[48,3200]{1,0:T(8,128)(2,1)S(1)}, bf16[48,3200]{1,0:T(8,128)(2,1)S(1)}, u32[]{:S(2)}, u32[]{:S(2)}) collective-permute-start(bf16[48,3200]{1,0:T(8,128)(2,1)S(1)} %get-tuple-element.177), channel_id=1, source_target_pairs={{0,2},{1,3},{2,0},{3,1},{4,6},{5,7},{6,4},{7,5},{8,10},{9,11},{10,... | collective-permute-start | bytes 921608 | tf_op jit(solution)/shard_map/ppermute | solution.py:680
  182.6 10.7 %collective-permute-start.38 = (bf16[2,96,768]{2,1,0:T(8,128)(2,1)S(1)}, bf16[2,96,768]{2,1,0:T(8,128)(2,1)S(1)}, u32[]{:S(2)}, u32[]{:S(2)}) collective-permute-start(bf16[2,96,768]{2,1,0:T(8,128)(2,1)S(1)} %get-tuple-element.191), channel_id=1, source_target_pairs={{0,4},{1,5},{2,6},{3,7},{4,0},{5,1},{6,2},{7,3},{8,12},{9,13},{10,... | collective-permute-start | bytes 884744 | tf_op jit(solution)/shard_map/ppermute | solution.py:680
  187.5 20.3 %collective-permute-start.35 = (bf16[48,3200]{1,0:T(8,128)(2,1)S(1)}, bf16[48,3200]{1,0:T(8,128)(2,1)}, u32[]{:S(2)}, u32[]{:S(2)}) collective-permute-start(bf16[48,3200]{1,0:T(8,128)(2,1)S(1)} %select_convert_fusion.2), channel_id=1, source_target_pairs={{0,8},{8,0},{16,24},{24,16},{1,9},{9,1},{17,25},{25,17},{2,10},{10... | collective-permute-start | bytes 921608 | tf_op jit(solution)/shard_map/ppermute | solution.py:764
  190.6 19.0 %collective-permute-start.39 = (bf16[192,768]{1,0:T(8,128)(2,1)}, bf16[192,768]{1,0:T(8,128)(2,1)}, u32[]{:S(2)}, u32[]{:S(2)}) collective-permute-start(bf16[192,768]{1,0:T(8,128)(2,1)} %add_convert_fusion.10), channel_id=1, source_target_pairs={{0,24},{24,0},{8,16},{16,8},{1,25},{25,1},{9,17},{17,9},{2,26},{26... | collective-permute-start | bytes 884744 | tf_op jit(solution)/shard_map/ppermute | solution.py:774
  196.0 30.1 %collective-permute-start.42 = (bf16[96,768]{1,0:T(8,128)(2,1)}, bf16[96,768]{1,0:T(8,128)(2,1)S(1)}, u32[]{:S(2)}, u32[]{:S(2)}) collective-permute-start(bf16[96,768]{1,0:T(8,128)(2,1)} %get-tuple-element.189), channel_id=1, source_target_pairs={{0,2},{1,3},{2,0},{3,1},{4,6},{5,7},{6,4},{7,5},{8,10},{9,11},{10,... | collective-permute-start | bytes 442376 | tf_op jit(solution)/shard_map/ppermute | solution.py:680
  196.5 29.6 %collective-permute-start.41 = (bf16[96,768]{1,0:T(8,128)(2,1)}, bf16[96,768]{1,0:T(8,128)(2,1)}, u32[]{:S(2)}, u32[]{:S(2)}) collective-permute-start(bf16[96,768]{1,0:T(8,128)(2,1)} %get-tuple-element.190), channel_id=1, source_target_pairs={{0,4},{1,5},{2,6},{3,7},{4,0},{5,1},{6,2},{7,3},{8,12},{9,13},{10,... | collective-permute-start | bytes 442376 | tf_op jit(solution)/shard_map/ppermute | solution.py:680
  210.8 19.7 %collective-permute-start.46 = (bf16[192,768]{1,0:T(8,128)(2,1)S(1)}, bf16[192,768]{1,0:T(8,128)(2,1)S(1)}, u32[]{:S(2)}, u32[]{:S(2)}) collective-permute-start(bf16[192,768]{1,0:T(8,128)(2,1)S(1)} %add_convert_fusion.9), channel_id=1, source_target_pairs={{0,8},{8,0},{16,24},{24,16},{1,9},{9,1},{17,25},{25,17},{2,10},{10... | collective-permute-start | bytes 884744 | tf_op jit(solution)/shard_map/ppermute | solution.py:780
  211.9 18.5 %collective-permute-start.40 = (bf16[48,3200]{1,0:T(8,128)(2,1)S(1)}, bf16[48,3200]{1,0:T(8,128)(2,1)S(1)}, u32[]{:S(2)}, u32[]{:S(2)}) collective-permute-start(bf16[48,3200]{1,0:T(8,128)(2,1)S(1)} %add_convert_fusion.5), channel_id=1, source_target_pairs={{0,24},{24,0},{8,16},{16,8},{1,25},{25,1},{9,17},{17,9},{2,26},{26... | collective-permute-start | bytes 921608 | tf_op jit(solution)/shard_map/ppermute | solution.py:774
  227.4 11.5 %collective-permute-start.44 = (bf16[192,768]{1,0:T(8,128)(2,1)S(1)}, bf16[192,768]{1,0:T(8,128)(2,1)S(1)}, u32[]{:S(2)}, u32[]{:S(2)}) collective-permute-start(bf16[192,768]{1,0:T(8,128)(2,1)S(1)} %pad_maximum_fusion.1), channel_id=1, source_target_pairs={{0,24},{24,0},{8,16},{16,8},{1,25},{25,1},{9,17},{17,9},{2,26},{26... | collective-permute-start | bytes 884744 | tf_op jit(solution)/shard_map/ppermute | solution.py:774
  230.6 12.8 %collective-permute-start.43 = (bf16[48,3200]{1,0:T(8,128)(2,1)S(1)}, bf16[48,3200]{1,0:T(8,128)(2,1)S(1)}, u32[]{:S(2)}, u32[]{:S(2)}) collective-permute-start(bf16[48,3200]{1,0:T(8,128)(2,1)S(1)} %add_convert_fusion.4), channel_id=1, source_target_pairs={{0,8},{8,0},{16,24},{24,16},{1,9},{9,1},{17,25},{25,17},{2,10},{10... | collective-permute-start | bytes 921608 | tf_op jit(solution)/shard_map/ppermute | solution.py:780
  (51 other events, 487.8 us)

commit v2 on v1

--- a/solution.py
+++ b/solution.py
@@ -235,34 +235,15 @@
             copy.wait()
 
 
-def ffn_kernel(counts, *refs):
-    inner_offsets, back_offsets = refs[:2]
-    inner_pieces = refs[2 : 2 + counts[0]]
-    back_pieces = refs[2 + counts[0] : 2 + counts[0] + counts[1]]
-    hidden, bias, vectors = refs[2 + sum(counts) : 5 + sum(counts)]
-    result, inner, back, act, inner_sems, back_sems = refs[-6:]
+def ffn_kernel(hidden, bias, vectors, inner, back, *rest):
+    result, act = rest[-2:]
     width = hidden.shape[1]
-    step = pl.program_id(0)
-
-    @pl.when(step == 0)
-    def _():
-        copies = start_pieces(inner_pieces, inner_offsets, inner, inner_sems)
-        start_pieces(back_pieces, back_offsets, back, back_sems)
-        for copy in copies:
-            copy.wait()
-
     x = hidden[...]
     low = x.astype(BF16)
     for c in range(inner.shape[1] // width):
         columns = slice(c * width, (c + 1) * width)
         value = mm(low, inner[:, columns]) + bias[:, columns]
         act[:, columns] = gelu_parts(value)[0].astype(BF16)
-
-    @pl.when(step == 0)
-    def _():
-        for copy in start_pieces(back_pieces, back_offsets, back, back_sems, started=True):
-            copy.wait()
-
     second = mm(act[...], back[...]) + vectors[5:6, :]
     normed, _ = norm_parts(x + second)
     result[...] = (normed * vectors[6:7, :] + vectors[7:8, :]).astype(BF16)
@@ -330,9 +311,10 @@
     back_pieces = refs[4 + counts[0] : 4 + sum(counts)]
     refs = refs[4 + sum(counts) :]
     compact_hbm, act_hbm, slope_hbm, vectors = refs[:4]
-    keep_back, send_back, keep_inner, send_inner, d_hidden_out, sums, inner_sum = refs[4:11]
-    back, inner, hidden, cotangent, act, slope, d_second, d_inner, d_hidden = refs[11:20]
-    total, out_back, out_inner, turned, ordered, inner_sems, back_sems, more = refs[20:]
+    inner_out, back_out = refs[4:6]
+    keep_back, send_back, keep_inner, send_inner, d_hidden_out, sums, inner_sum = refs[6:13]
+    back, inner, hidden, cotangent, act, slope, d_second, d_inner, d_hidden = refs[13:22]
+    total, out_back, out_inner, turned, ordered, inner_sems, back_sems, more = refs[22:]
     width = inner.shape[0]
     size = inner.shape[1] // BLOCKS
     quarters = inner.shape[1] // width
@@ -372,6 +354,11 @@
 
     for copy in back_copies:
         copy.wait()
+    exports = [
+        pltpu.make_async_copy(back, back_out, back_sems.at[0]),
+        pltpu.make_async_copy(inner, inner_out, inner_sems.at[0]),
+    ]
+    exports[0].start()
 
     @pl.loop(0, count_live)
     def _(b):
@@ -412,6 +399,7 @@
         outs[-1].start()
     for copy in inner_copies:
         copy.wait()
+    exports[1].start()
 
     @pl.loop(0, count_live)
     def _(b):
@@ -474,7 +462,7 @@
         hidden_copy(b).start()
         hidden_copy(b).wait()
 
-    for copy in outs:
+    for copy in outs + exports:
         copy.wait()
 
 
@@ -706,10 +694,9 @@
 
 
 class Sum:
-    def __init__(self, keep, send, early=False):
-        self.keep, self.early = keep, early
+    def __init__(self, keep, send):
+        self.keep = keep
         self.got = swap(send, CORE)
-        self.extra = None
         z = lax.axis_index("rep")
         self.ends = (z == 0) | (z == 3)
 
@@ -720,26 +707,12 @@
             setattr(self, name, value)
 
     def chip(self, block, bottom):
-        if self.early:
-            half = self.mine.shape[1] // 2
-            rows = slice(half, None) if bottom else slice(0, half)
-            return self.mine[block, rows].astype(F32) + self.extra[block, rows].astype(F32)
         half = self.keep.shape[1] // 2
         rows = slice(half, None) if bottom else slice(0, half)
         return self.keep[block, rows].astype(F32) + self.got[block, rows].astype(F32)
 
-    def rep_early(self, *others):
+    def near(self, *others):
         self.wait(("keep", "got"), others)
-        half = self.keep.shape[1] // 2
-        a = self.keep[:, :half].astype(F32) + self.got[:, :half].astype(F32)
-        b = self.keep[:, half:].astype(F32) + self.got[:, half:].astype(F32)
-        sent = jnp.where(self.ends, b, a).astype(BF16)
-        self.mine = jnp.where(self.ends, a, b).astype(BF16)
-        self.extra = lax.ppermute(sent, "rep", PAIRS)
-        return (sent,)
-
-    def near(self, *others):
-        self.wait(("mine", "extra") if self.early else ("keep", "got"), others)
         sent = self.chip(slice(1, 3), False).astype(BF16), self.chip(slice(2, 4), True).astype(BF16)
         self.got_a, self.got_b = swap(sent[0], XBIT), swap(sent[1], YBIT)
         return sent
@@ -760,17 +733,13 @@
         self.wait(("far_a", "far_b"), others)
         a, b = self.halves()
         sent = jnp.where(self.ends, b, a).astype(BF16)
-        self.total = jnp.where(self.ends, a, b).astype(BF16)
         self.across = lax.ppermute(sent, "rep", PAIRS)
         return (sent,)
 
     def rep_second(self, *others):
-        if self.early:
-            self.wait(("far_a", "far_b"), others)
-            self.total = jnp.concatenate(self.halves(), 0).astype(BF16)
-        else:
-            self.wait(("across",), others)
-            self.total = (self.total.astype(F32) + self.across.astype(F32)).astype(BF16)
+        self.wait(("across",), others)
+        a, b = self.halves()
+        self.total = (jnp.where(self.ends, a, b) + self.across.astype(F32)).astype(BF16)
         self.across = lax.ppermute(self.total, "rep", ACROSS)
         return (self.total,)
 
@@ -786,6 +755,42 @@
         return jnp.concatenate([top, bottom], 0).astype(F32)
 
 
+class EarlySum(Sum):
+    def part(self, start, stop, other=False):
+        half = self.keep.shape[1] // 2
+        first = jnp.where(self.ends == other, half, 0)
+        return sum(
+            lax.dynamic_slice(v, (start, first, 0), (stop - start, half, v.shape[2])).astype(F32)
+            for v in (self.keep, self.got)
+        )
+
+    def rep_early(self, *others):
+        self.wait(("keep", "got"), others)
+        sent = self.part(0, 4, other=True).astype(BF16)
+        self.extra = lax.ppermute(sent, "rep", PAIRS)
+        return (sent,)
+
+    def near(self, *others):
+        self.wait(("keep", "got", "extra"), others)
+        sent = (self.part(1, 3) + self.extra[1:3].astype(F32)).astype(BF16)
+        self.got_a = swap(sent, XBIT)
+        return (sent,)
+
+    def far(self, *others):
+        self.wait(("got_a",), others)
+        sent = self.part(3, 4)[0] + self.extra[3].astype(F32) + self.got_a[1].astype(F32)
+        sent = sent.astype(BF16)
+        self.far_a = swap(sent, YBIT)
+        return (sent,)
+
+    def rep_second(self, *others):
+        self.wait(("far_a",), others)
+        total = self.part(0, 1)[0] + self.extra[0].astype(F32) + self.got_a[0].astype(F32)
+        self.total = (total + self.far_a.astype(F32)).astype(BF16)
+        self.across = lax.ppermute(self.total, "rep", ACROSS)
+        return (self.total,)
+
+
 PAIRS = [(0, 1), (1, 0), (2, 3), (3, 2)]
 ACROSS = [(0, 3), (3, 0), (1, 2), (2, 1)]
 
@@ -807,8 +812,8 @@
     return jax.ShapeDtypeStruct(dims, dtype)
 
 
-def params():
-    return pltpu.CompilerParams(vmem_limit_bytes=VMEM)
+def params(limit=VMEM):
+    return pltpu.CompilerParams(vmem_limit_bytes=limit)
 
 
 def cost(time):
@@ -1002,11 +1007,13 @@
     half = BLOCKS // 2
     size = hidden // BLOCKS
     block = width // BLOCKS
-    keep_back, send_back, keep_inner, send_inner, d_hidden1, sums, inner_sum = pl.pallas_call(
+    inner_full, back_full, keep_back, send_back, keep_inner, send_inner, d_hidden1, sums, inner_sum = pl.pallas_call(
         functools.partial(ffn_back_kernel, (inner_count, back_count)),
         in_specs=[SCALARS] * 4 + [ANYWHERE] * (inner_count + back_count + 3) + [in_vmem],
-        out_specs=[ANYWHERE] * 5 + [in_vmem] * 2,
+        out_specs=[ANYWHERE] * 7 + [in_vmem] * 2,
         out_shape=[
+            shape_of(width, hidden),
+            shape_of(hidden, width),
             shape_of(half, size, width),
             shape_of(half, size, width),
             shape_of(half, size, width),
@@ -1052,7 +1059,7 @@
 
     if cube:
         back_total = Sum(keep_back, send_back)
-        inner_total = Sum(keep_inner, send_inner, early=True)
+        inner_total = EarlySum(keep_inner, send_inner)
 
     d_qkv, d_r1, keep_attn, send_attn = pl.pallas_call(
         functools.partial(attend_back_kernel, attn_count, seq, rows),
@@ -1111,37 +1118,21 @@
     def later(shift):
         return lambda i: (i + shift, 0)
 
-    def ffn(first, x, *done):
+    def ffn(first, number, x, *done):
         return pl.pallas_call(
-            functools.partial(ffn_kernel, (inner_count, back_count)),
-            grid=(grid[0] // 2,),
-            in_specs=[SCALARS] * 2
-            + [ANYWHERE] * (inner_count + back_count)
-            + [pl.BlockSpec((STEP, width), later(first)), whole((1, hidden)), whole((16, width))]
+            ffn_kernel,
+            grid=(number,),
+            in_specs=[pl.BlockSpec((STEP, width), later(first)), whole((1, hidden)), whole((16, width))]
+            + [in_vmem] * 2
             + [ANYWHERE] * len(done),
             out_specs=pl.BlockSpec((STEP, width), later(first)),
             out_shape=shape_of(count, width),
-            input_output_aliases={5 + inner_count + back_count: 0} if done else {},
-            scratch_shapes=[
-                pltpu.VMEM((width, hidden), BF16),
-                pltpu.VMEM((hidden, width), BF16),
-                pltpu.VMEM((STEP, hidden), BF16),
-                pltpu.SemaphoreType.DMA((inner_count,)),
-                pltpu.SemaphoreType.DMA((back_count,)),
-            ],
-            compiler_params=params(),
+            input_output_aliases={5: 0} if done else {},
+            scratch_shapes=[pltpu.VMEM((STEP, hidden), BF16)],
+            compiler_params=params(24 * 2**20),
             cost_estimate=cost(11),
             name="ffn",
-        )(
-            inner_offsets,
-            back_offsets,
-            *inner_pieces,
-            *back_pieces,
-            x,
-            inner_bias_full,
-            vector_rows,
-            *done,
-        )
+        )(x, inner_bias_full, vector_rows, inner_full, back_full, *done)
 
     x = hidden1
     if cube:
@@ -1150,7 +1141,7 @@
         attn_total = Sum(keep_attn, send_attn)
         sent += attn_total.near(*sent)
         x = after(hidden1, *sent)
-    result = ffn(0, x)
+    result = ffn(0, grid[0] - 1, x)
     if cube:
         sent = back_total.far(result)
         sent += attn_total.far(*sent)
@@ -1158,7 +1149,6 @@
         sent += inner_total.near(*sent)
         sent += attn_total.rep_first(*sent)
         sent += back_total.rep_second(*sent)
-        sent += inner_total.far(*sent)
         d_qkv = after(d_qkv, *sent)
 
     input_grad = pl.pallas_call(
@@ -1173,16 +1163,17 @@
             pltpu.VMEM((width, 3 * width), BF16),
             pltpu.SemaphoreType.DMA((attn_count,)),
         ],
-        compiler_params=params(),
+        compiler_params=params(24 * 2**20),
         cost_estimate=cost(9),
         name="input_grad",
     )(attn_offsets, base, *attn_pieces, d_qkv, d_r1, pos)
 
     if cube:
         sent = attn_total.rep_second(input_grad)
+        sent += inner_total.far(*sent)
         sent += back_total.rep_third(*sent)
         x = after(hidden1, *sent)
-    result = ffn(grid[0] // 2, x, result)
+    result = ffn(grid[0] - 1, 1, x, result)
     if cube:
         sent = inner_total.rep_second(result)
 

time: 255 us -> 240 us (0.941)
  Pallas kernels: 122 us -> 107 us
  starting transfers between devices: 42.1 us -> 50 us
  waiting for transfers between devices: 40.8 us -> 33.3 us
  other arithmetic: 33 us -> 29.3 us
  local copies, waits for them, and re-layouts: 9.99 us -> 13.4 us
    pallas_call x2, Pallas kernels: 26.8 us -> 14.1 us  [ffn(): pl.pallas_call(ffn_kernel, grid=(number,), in_specs=[pl.BlockSpec((STEP,...]
    ppermute x3, starting transfers between devices: 2.71 us -> 8.22 us  [rep_third(): self.other = lax.ppermute(self.low, 'rep', PAIRS)]
    ppermute x3, waiting for transfers between devices: 7.21 us -> 3.47 us  [rep_second(): self.across = lax.ppermute(self.total, 'rep', ACROSS)]
    unnamed x72 -> x112, local copies, waits for them, and re-layouts: 4.77 us -> 8.16 us
    ppermute x3, starting transfers between devices: 6.59 us -> 9.3 us  [rep_second(): self.across = lax.ppermute(self.total, 'rep', ACROSS)]
    convert_element_type x3 -> x6, other arithmetic: 7.7 us -> 9.68 us  [the longest x2 3.24 us: rep_second(): (jnp.where(self.ends, a, b) + self.across.astype(F32)).astype(BF16)]
    ppermute x38 -> x36, waiting for transfers between devices: 28.8 us -> 26.9 us  [swap(): return lax.ppermute(value, 'shard', [(i, i ^ bit) for i in range(8)])]
    convert_element_type x3 -> x2, other arithmetic: 6.49 us -> 5.52 us  [near(): self.chip(slice(2, 4), True).astype(BF16)]
  transfers between devices with their start and end apart: 47 -> 45, of which waited for: 15 -> 14; matrix products, arithmetic and copies ran while one was open for 14% -> 13% of each run, Pallas kernels for 42% -> 38%
where the time goes in v2:
time: 240 us; the launch traced here: 235 us
  Pallas kernels  107 us (45%)
  starting transfers between devices  50 us (21%)
  waiting for transfers between devices  33.3 us (14%)
  other arithmetic  29.3 us (12%)
  local copies, waits for them, and re-layouts  13.4 us (6%)
  between operations  2.41 us (1%)
    pallas_call x1, Pallas kernels, local(): pl.pallas_call(functools.partial(attend_back_kernel, attn_count, seq, row...  31.6 us
    ppermute x36, starting transfers between devices, swap(): return lax.ppermute(value, 'shard', [(i, i ^ bit) for i in range(8)])  29.1 us
    ppermute x36, waiting for transfers between devices, swap(): return lax.ppermute(value, 'shard', [(i, i ^ bit) for i in range(8)])  26.9 us
    pallas_call x1, Pallas kernels, local(): pl.pallas_call(functools.partial(ffn_back_kernel, (inner_count, back_coun...  16.8 us
    pallas_call x2, Pallas kernels, ffn(): pl.pallas_call(ffn_kernel, grid=(number,), in_specs=[pl.BlockSpec((STEP,...  14.1 us
    pallas_call x1, Pallas kernels, local(): pl.pallas_call(functools.partial(settle_kernel, attn_count, seq), grid=gr...  10.3 us
    pallas_call x1, Pallas kernels, local(): pl.pallas_call(functools.partial(project_kernel, attn_count, rows), grid=...  9.76 us
    pallas_call x1, Pallas kernels, local(): pl.pallas_call(functools.partial(attend_kernel, seq), grid=grid, in_specs...  9.62 us
  transfers between devices with their start and end apart: 45, of which 14 were waited for; matrix products, arithmetic and copies ran while one was open for 13% of the time, Pallas kernels for 38%

profile of v2, /device:TPU:0, one launch (start us, length us, event | category | flops | bytes accessed | tf_op | source)
XLA Modules:
  0.0 235.5 jit_solution(9990393204753347276)
XLA Ops:
  3.8 3.0 %collective-permute-start = (bf16[96,3200]{1,0:T(8,128)(2,1)S(1)}, bf16[96,3200]{1,0:T(8,128)(2,1)S(1)}, u32[]{:S(2)}, u32[]{:S(2)}) collective-permute-start(bf16[96,3200]{1,0:T(8,128)(2,1)S(1)} %fusion.1.refs_1_.refs_2_.refs_6_), channel_id=1, source_target_pairs={{0,2},{1,3},{2,0},{3,1},{4,6},{5,7},{6,4},{7,5},{8,10},{9,11},{10,... | collective-permute-start | bytes 1843208 | tf_op jit(solution)/shard_map/ppermute | solution.py:668
  13.3 7.3 %collective-permute-done.refs_2_.refs_3_.refs_7_ = bf16[96,3200]{1,0:T(8,128)(2,1)S(1)} collective-permute-done((bf16[96,3200]{1,0:T(8,128)(2,1)S(1)}, bf16[96,3200]{1,0:T(8,128)(2,1)S(1)}, u32[]{:S(2)}, u32[]{:S(2)}) %collective-permute-start) | collective-permute-done | bytes 614432 | tf_op jit(solution)/shard_map/ppermute | solution.py:668
  23.1 1.8 collective-permute-start.8
  26.4 6.5 %collective-permute-done.7.refs_4_.refs_5_.refs_9_ = bf16[48,3200]{1,0:T(8,128)(2,1)S(1)} collective-permute-done((bf16[48,3200]{1,0:T(8,128)(2,1)S(1)}, bf16[48,3200]{1,0:T(8,128)(2,1)S(1)}, u32[]{:S(2)}, u32[]{:S(2)}) %collective-permute-start.7) | collective-permute-done | bytes 307232 | tf_op jit(solution)/shard_map/ppermute | solution.py:668
  38.6 9.8 %project.1 = (bf16[1024,2304]{1,0:T(8,128)(2,1)}, f32[16,768]{1,0:T(8,128)}, f32[1,3072]{1,0:T(1,128)}) custom-call(s32[10]{0:T(128)} %pad_add_fusion.1.refs_0_, bf16[96,3200]{1,0:T(8,128)(2,1)} %copy-done.2, bf16[96,3200]{1,0:T(8,128)(2,1)} %copy-done.5, bf16[96,3200]{1,0:T(8,128)(2,1)} %copy-done.7, bf16[48,3200]{1,0:T(8,128)(2,1)} %copy-done.15, ...), custom_call_target="tpu_custom_call" | custom-call | flops 900000000 | tf_op jit(solution)/shard_map/project/pallas_call | solution.py:918
  50.3 9.6 %attend.1.refs_14_ = bf16[1024,768]{1,0:T(8,128)(2,1)} custom-call(s32[8]{0:T(128)} %refs_3_.1, s32[8]{0:T(128)} %refs_4_.2, bf16[1024,2304]{1,0:T(8,128)(2,1)} %get-tuple-element.105.qkv.refs_18_), custom_call_target="tpu_custom_call" | custom-call | flops 800000000 | tf_op jit(solution)/shard_map/attend/pallas_call | solution.py:940
  60.0 1.8 collective-permute-start.18
  62.3 10.3 %settle.1 = (f32[1024,768]{1,0:T(8,128)}, bf16[768,3200]{1,0:T(8,128)(2,1)}) custom-call(s32[10]{0:T(128)} %pad_add_fusion.1.refs_0_, s32[9]{0:T(128)} %copy-done.26, bf16[96,3200]{1,0:T(8,128)(2,1)} %copy-done.2, bf16[96,3200]{1,0:T(8,128)(2,1)} %copy-done.5, bf16[96,3200]{1,0:T(8,128)(2,1)} %copy-done.7, bf16[48,3200]{1,0:T(8,128)(2,1)} %copy-done.15, ...), custom_call_target="tpu_custom_call" | custom-call | flops 900000000 | tf_op jit(solution)/shard_map/settle/pallas_call | solution.py:956
  72.6 2.6 %collective-permute-done.18.refs_15_ = bf16[384,768]{1,0:T(8,128)(2,1)S(1)} collective-permute-done((bf16[384,768]{1,0:T(8,128)(2,1)}, bf16[384,768]{1,0:T(8,128)(2,1)S(1)}, u32[]{:S(2)}, u32[]{:S(2)}) %collective-permute-start.18) | collective-permute-done | bytes 589856 | tf_op jit(solution)/shard_map/ppermute | solution.py:668
  78.1 6.6 %live_inner.1 = (bf16[768,3072]{1,0:T(8,128)(2,1)}, bf16[768,3072]{1,0:T(8,128)(2,1)}) custom-call(s32[8]{0:T(128)} %get-tuple-element.117.refs_0_, s32[1]{0:T(128)S(6)} %max.3.refs_1_.refs_3_.refs_5_, bf16[96,3072]{1,0:T(8,128)(2,1)} %refs_4_.1, bf16[96,3072]{1,0:T(8,128)(2,1)} %collective-permute-done.5.refs_3_.refs_5_, ...), custom_call_target="tpu_custom_call" | custom-call | flops 600000000 | tf_op jit(solution)/shard_map/live_inner/pallas_call | solution.py:983
  85.6 16.8 %ffn_back.1 = (bf16[768,3072]{1,0:T(8,128)(2,1)}, bf16[3072,768]{1,0:T(8,128)(2,1)}, bf16[4,384,768]{2,1,0:T(8,128)(2,1)}, bf16[4,384,768]{2,1,0:T(8,128)(2,1)},...) custom-call(s32[8]{0:T(128)} %get-tuple-element.117.refs_0_, ...), custom_call_target="tpu_custom_call" | custom-call | flops 1300000000 | tf_op jit(solution)/shard_map/ffn_back/pallas_call | solution.py:1010
  103.0 31.6 %attend_back.1 = (bf16[1024,2304]{1,0:T(8,128)(2,1)}, bf16[768,768]{1,0:T(8,128)(2,1)}, bf16[4,96,3200]{2,1,0:T(8,128)(2,1)}, bf16[4,96,3200]{2,1,0:T(8,128)(2,1)}) custom-call(s32[10]{0:T(128)} %pad_add_fusion.1.refs_0_, s32[8]{0:T(128)} %broadcast_xor_fusion.refs_2_.refs_1_, s32[9]{0:T(128)} %copy-done.26, s32[8]{0:T(128)} %refs_3_.1, s32[8]{0:T(128)} %refs_4_.2, ...), custom_call_target="tpu_custom_call" | custom-call | flops 2200000000 | tf_op jit(solution)/shard_map/attend_back/pallas_call | solution.py:1064
  134.8 2.7 %add_convert_fusion.4 = (bf16[2,192,768]{2,1,0:T(8,128)(2,1)}, bf16[2,192,768]{2,1,0:T(8,128)(2,1)}) fusion(bf16[4,384,768]{2,1,0:T(8,128)(2,1)} %collective-permute-done.24, bf16[4,384,768]{2,1,0:T(8,128)(2,1)S(1)} %copy-done.30), kind=kLoop, calls=%fused_computation.7 | loop fusion | flops 2359296 | bytes 3538944 | tf_op jit(solution)/shard_map/convert_element_type | solution.py:716
  137.5 1.7 collective-permute-start.28
  140.7 2.8 %add_convert_fusion = bf16[4,192,768]{2,1,0:T(8,128)(2,1)} fusion(bf16[4,384,768]{2,1,0:T(8,128)(2,1)} %collective-permute-done.25, s32[]{:T(128)S(6)} %select_n.94, bf16[4,384,768]{2,1,0:T(8,128)(2,1)S(1)} %copy-done.32), kind=kLoop, calls=%fused_computation | loop fusion | flops 2359296 | bytes 3538948 | tf_op jit(solution)/shard_map/convert_element_type | solution.py:769
  143.5 2.8 %add_convert_fusion.1 = (bf16[2,48,3200]{2,1,0:T(8,128)(2,1)}, bf16[2,48,3200]{2,1,0:T(8,128)(2,1)}) fusion(bf16[4,96,3200]{2,1,0:T(8,128)(2,1)} %collective-permute-done.23, bf16[4,96,3200]{2,1,0:T(8,128)(2,1)S(1)} %copy-done.28), kind=kLoop, calls=%fused_computation.2 | loop fusion | flops 2457600 | bytes 3686400 | tf_op jit(solution)/shard_map/convert_element_type | solution.py:716
  147.1 1.8 collective-permute-start.34
  148.9 2.3 copy-done
  151.3 2.3 copy-done.1
  153.6 10.3 %ffn.2.rest_0_ = bf16[1024,768]{1,0:T(8,128)(2,1)} custom-call(f32[1024,768]{1,0:T(8,128)S(1)} %copy-done.4, f32[1,3072]{1,0:T(1,128)S(1)} %copy-done.23, f32[16,768]{1,0:T(8,128)S(1)} %copy-done.21, bf16[768,3072]{1,0:T(8,128)(2,1)S(1)} %copy-done, bf16[3072,768]{1,0:T(8,128)(2,1)S(1)} %copy-done.1), custom_call_target="tpu_custom_call" | custom-call | flops 1100000000 | tf_op jit(solution)/shard_map/ffn/pallas_call | solution.py:1122
  171.7 3.7 %collective-permute-done.32 = bf16[192,768]{1,0:T(8,128)(2,1)S(1)} collective-permute-done((bf16[192,768]{1,0:T(8,128)(2,1)S(1)}, bf16[192,768]{1,0:T(8,128)(2,1)S(1)}, u32[]{:S(2)}, u32[]{:S(2)}) %collective-permute-start.32) | collective-permute-done | bytes 294944 | tf_op jit(solution)/shard_map/ppermute | solution.py:668
  179.7 1.9 collective-permute-start.37
  182.2 1.7 select_convert_fusion
  187.1 2.8 %collective-permute-start.38 = (bf16[192,768]{1,0:T(8,128)(2,1)S(1)}, bf16[192,768]{1,0:T(8,128)(2,1)S(1)}, u32[]{:S(2)}, u32[]{:S(2)}) collective-permute-start(bf16[192,768]{1,0:T(8,128)(2,1)S(1)} %add_convert_fusion.13), channel_id=1, source_target_pairs={{0,24},{24,0},{8,16},{16,8},{1,25},{25,1},{9,17},{17,9},{2,26},{26... | collective-permute-start | bytes 884744 | tf_op jit(solution)/shard_map/ppermute | solution.py:743
  190.1 8.4 %input_grad.1 = f32[1024,768]{1,0:T(8,128)} custom-call(s32[10]{0:T(128)S(1)} %copy-done.25, s32[9]{0:T(128)S(1)} %copy-done.27, bf16[96,3200]{1,0:T(8,128)(2,1)S(1)} %copy-done.3, bf16[96,3200]{1,0:T(8,128)(2,1)S(1)} %copy-done.6, bf16[96,3200]{1,0:T(8,128)(2,1)S(1)} %copy-done.8, bf16[48,3200]{1,0:T(8,128)(2,1)S(1)} %copy-done.16, ...), custom_call_target="tpu_custom_call" | custom-call | flops 900000000 | tf_op jit(solution)/shard_map/input_grad/pallas_call | solution.py:1154
  200.1 2.6 %collective-permute-start.39 = (bf16[48,3200]{1,0:T(8,128)(2,1)S(1)}, bf16[48,3200]{1,0:T(8,128)(2,1)S(1)}, u32[]{:S(2)}, u32[]{:S(2)}) collective-permute-start(bf16[48,3200]{1,0:T(8,128)(2,1)S(1)} %add_convert_fusion.7), channel_id=1, source_target_pairs={{0,24},{24,0},{8,16},{16,8},{1,25},{25,1},{9,17},{17,9},{2,26},{26... | collective-permute-start | bytes 921608 | tf_op jit(solution)/shard_map/ppermute | solution.py:743
  206.7 3.9 %ffn.3 = bf16[1024,768]{1,0:T(8,128)(2,1)} custom-call(f32[1024,768]{1,0:T(8,128)S(1)} %copy-done.4, f32[1,3072]{1,0:T(1,128)S(1)} %copy-done.23, f32[16,768]{1,0:T(8,128)S(1)} %copy-done.21, bf16[768,3072]{1,0:T(8,128)(2,1)S(1)} %bitcast.72, bf16[3072,768]{1,0:T(8,128)(2,1)S(1)} %bitcast.74, ...), custom_call_target="tpu_custom_call", output_to_operand_aliasing={{}: (5, {})} | custom-call | flops 1100000000 | tf_op jit(solution)/shard_map/ffn/pallas_call | solution.py:1122
  211.8 3.9 %collective-permute-start.42 = (bf16[192,768]{1,0:T(8,128)(2,1)S(1)}, bf16[192,768]{1,0:T(8,128)(2,1)S(1)}, u32[]{:S(2)}, u32[]{:S(2)}) collective-permute-start(bf16[192,768]{1,0:T(8,128)(2,1)S(1)} %fusion.2), channel_id=1, source_target_pairs={{0,24},{24,0},{8,16},{16,8},{1,25},{25,1},{9,17},{17,9},{2,26},{26... | collective-permute-start | bytes 884744 | tf_op jit(solution)/shard_map/ppermute | solution.py:790
  215.8 4.0 %collective-permute-start.41 = (bf16[48,3200]{1,0:T(8,128)(2,1)S(1)}, bf16[48,3200]{1,0:T(8,128)(2,1)S(1)}, u32[]{:S(2)}, u32[]{:S(2)}) collective-permute-start(bf16[48,3200]{1,0:T(8,128)(2,1)S(1)} %add_convert_fusion.6), channel_id=1, source_target_pairs={{0,8},{8,0},{16,24},{24,16},{1,9},{9,1},{17,25},{25,17},{2,10},{10... | collective-permute-start | bytes 921608 | tf_op jit(solution)/shard_map/ppermute | solution.py:749
  221.0 3.5 %collective-permute-done.42 = bf16[192,768]{1,0:T(8,128)(2,1)S(1)} collective-permute-done((bf16[192,768]{1,0:T(8,128)(2,1)S(1)}, bf16[192,768]{1,0:T(8,128)(2,1)S(1)}, u32[]{:S(2)}, u32[]{:S(2)}) %collective-permute-start.42) | collective-permute-done | bytes 294944 | tf_op jit(solution)/shard_map/ppermute | solution.py:790
  224.5 2.9 %collective-permute-start.43 = (bf16[192,768]{1,0:T(8,128)(2,1)S(1)}, bf16[192,768]{1,0:T(8,128)(2,1)S(1)}, u32[]{:S(2)}, u32[]{:S(2)}) collective-permute-start(bf16[192,768]{1,0:T(8,128)(2,1)S(1)} %add_convert_fusion.10), channel_id=1, source_target_pairs={{0,8},{8,0},{16,24},{24,16},{1,9},{9,1},{17,25},{25,17},{2,10},{10... | collective-permute-start | bytes 884744 | tf_op jit(solution)/shard_map/ppermute | solution.py:749
  231.2 2.8 %collective-permute-done.43 = bf16[192,768]{1,0:T(8,128)(2,1)S(1)} collective-permute-done((bf16[192,768]{1,0:T(8,128)(2,1)S(1)}, bf16[192,768]{1,0:T(8,128)(2,1)S(1)}, u32[]{:S(2)}, u32[]{:S(2)}) %collective-permute-start.43) | collective-permute-done | bytes 294944 | tf_op jit(solution)/shard_map/ppermute | solution.py:749
  (238 shorter events, 56.7 us)
Async XLA Ops:
  3.8 16.9 %collective-permute-start = (bf16[96,3200]{1,0:T(8,128)(2,1)S(1)}, bf16[96,3200]{1,0:T(8,128)(2,1)S(1)}, u32[]{:S(2)}, u32[]{:S(2)}) collective-permute-start(bf16[96,3200]{1,0:T(8,128)(2,1)S(1)} %fusion.1.refs_1_.refs_2_.refs_6_), channel_id=1, source_target_pairs={{0,2},{1,3},{2,0},{3,1},{4,6},{5,7},{6,4},{7,5},{8,10},{9,11},{10,... | collective-permute-start | bytes 1843208 | tf_op jit(solution)/shard_map/ppermute | solution.py:668
  6.8 15.3 %collective-permute-start.1 = (bf16[96,3200]{1,0:T(8,128)(2,1)S(1)}, bf16[96,3200]{1,0:T(8,128)(2,1)S(1)}, u32[]{:S(2)}, u32[]{:S(2)}) collective-permute-start(bf16[96,3200]{1,0:T(8,128)(2,1)S(1)} %fusion.1.refs_1_.refs_2_.refs_6_), channel_id=1, source_target_pairs={{0,4},{1,5},{2,6},{3,7},{4,0},{5,1},{6,2},{7,3},{8,12},{9,13},{10,... | collective-permute-start | bytes 1843208 | tf_op jit(solution)/shard_map/ppermute | solution.py:668
  8.3 13.8 %collective-permute-start.2 = (bf16[96,3200]{1,0:T(8,128)(2,1)S(1)}, bf16[96,3200]{1,0:T(8,128)(2,1)S(1)}, u32[]{:S(2)}, u32[]{:S(2)}) collective-permute-start(bf16[96,3200]{1,0:T(8,128)(2,1)S(1)} %fusion.1.refs_1_.refs_2_.refs_6_), channel_id=1, source_target_pairs={{0,1},{1,0},{2,3},{3,2},{4,5},{5,4},{6,7},{7,6},{8,9},{9,8},{10,11... | collective-permute-start | bytes 1843208 | tf_op jit(solution)/shard_map/ppermute | solution.py:668
  22.1 12.3 %collective-permute-start.9 = (bf16[96,3200]{1,0:T(8,128)(2,1)S(1)}, bf16[96,3200]{1,0:T(8,128)(2,1)S(1)}, u32[]{:S(2)}, u32[]{:S(2)}) collective-permute-start(bf16[96,3200]{1,0:T(8,128)(2,1)S(1)} %collective-permute-done.refs_2_.refs_3_.refs_7_), channel_id=1, source_target_pairs={{0,1},{1,0},{2,3},{3,2},{4,5},{5,4},{6,7},{7,6},{8,9},{9,8},{10,11... | collective-permute-start | bytes 1843208 | tf_op jit(solution)/shard_map/ppermute | solution.py:668
  22.2 12.3 %collective-permute-start.10 = (bf16[96,3200]{1,0:T(8,128)(2,1)S(1)}, bf16[96,3200]{1,0:T(8,128)(2,1)S(1)}, u32[]{:S(2)}, u32[]{:S(2)}) collective-permute-start(bf16[96,3200]{1,0:T(8,128)(2,1)S(1)} %collective-permute-done.1.refs_3_.refs_4_.refs_8_), channel_id=1, source_target_pairs={{0,1},{1,0},{2,3},{3,2},{4,5},{5,4},{6,7},{7,6},{8,9},{9,8},{10,11... | collective-permute-start | bytes 1843208 | tf_op jit(solution)/shard_map/ppermute | solution.py:668
  23.1 11.3 %collective-permute-start.8 = (bf16[48,3200]{1,0:T(8,128)(2,1)S(1)}, bf16[48,3200]{1,0:T(8,128)(2,1)S(1)}, u32[]{:S(2)}, u32[]{:S(2)}) collective-permute-start(bf16[48,3200]{1,0:T(8,128)(2,1)S(1)} %slice.203), channel_id=1, source_target_pairs={{0,4},{1,5},{2,6},{3,7},{4,0},{5,1},{6,2},{7,3},{8,12},{9,13},{10,... | collective-permute-start | bytes 921608 | tf_op jit(solution)/shard_map/ppermute | solution.py:668
  24.9 23.5 %collective-permute-start.5 = (bf16[96,3072]{1,0:T(8,128)(2,1)}, bf16[96,3072]{1,0:T(8,128)(2,1)}, u32[]{:S(2)}, u32[]{:S(2)}) collective-permute-start(bf16[96,3072]{1,0:T(8,128)(2,1)} %refs_4_.1), channel_id=1, source_target_pairs={{0,2},{1,3},{2,0},{3,1},{4,6},{5,7},{6,4},{7,5},{8,10},{9,11},{10,... | collective-permute-start | bytes 1769480 | tf_op jit(solution)/shard_map/ppermute | solution.py:668
  32.9 16.6 %collective-permute-start.6 = (bf16[96,3072]{1,0:T(8,128)(2,1)}, bf16[96,3072]{1,0:T(8,128)(2,1)}, u32[]{:S(2)}, u32[]{:S(2)}) collective-permute-start(bf16[96,3072]{1,0:T(8,128)(2,1)} %refs_4_.1), channel_id=1, source_target_pairs={{0,4},{1,5},{2,6},{3,7},{4,0},{5,1},{6,2},{7,3},{8,12},{9,13},{10,... | collective-permute-start | bytes 1769480 | tf_op jit(solution)/shard_map/ppermute | solution.py:668
  35.8 24.1 %collective-permute-start.14 = (bf16[384,768]{1,0:T(8,128)(2,1)}, bf16[384,768]{1,0:T(8,128)(2,1)}, u32[]{:S(2)}, u32[]{:S(2)}) collective-permute-start(bf16[384,768]{1,0:T(8,128)(2,1)} %refs_12_.2), channel_id=1, source_target_pairs={{0,2},{1,3},{2,0},{3,1},{4,6},{5,7},{6,4},{7,5},{8,10},{9,11},{10,... | collective-permute-start | bytes 1769480 | tf_op jit(solution)/shard_map/ppermute | solution.py:668
  38.1 21.9 %collective-permute-start.15 = (bf16[384,768]{1,0:T(8,128)(2,1)}, bf16[384,768]{1,0:T(8,128)(2,1)}, u32[]{:S(2)}, u32[]{:S(2)}) collective-permute-start(bf16[384,768]{1,0:T(8,128)(2,1)} %refs_12_.2), channel_id=1, source_target_pairs={{0,4},{1,5},{2,6},{3,7},{4,0},{5,1},{6,2},{7,3},{8,12},{9,13},{10,... | collective-permute-start | bytes 1769480 | tf_op jit(solution)/shard_map/ppermute | solution.py:668
  49.5 10.5 %collective-permute-start.16 = (bf16[96,3072]{1,0:T(8,128)(2,1)}, bf16[96,3072]{1,0:T(8,128)(2,1)S(1)}, u32[]{:S(2)}, u32[]{:S(2)}) collective-permute-start(bf16[96,3072]{1,0:T(8,128)(2,1)} %collective-permute-done.5.refs_3_.refs_5_), channel_id=1, source_target_pairs={{0,1},{1,0},{2,3},{3,2},{4,5},{5,4},{6,7},{7,6},{8,9},{9,8},{10,11... | collective-permute-start | bytes 1769480 | tf_op jit(solution)/shard_map/ppermute | solution.py:668
  49.5 10.5 %collective-permute-start.17 = (bf16[96,3072]{1,0:T(8,128)(2,1)}, bf16[96,3072]{1,0:T(8,128)(2,1)S(1)}, u32[]{:S(2)}, u32[]{:S(2)}) collective-permute-start(bf16[96,3072]{1,0:T(8,128)(2,1)} %collective-permute-done.6.refs_4_.refs_6_), channel_id=1, source_target_pairs={{0,1},{1,0},{2,3},{3,2},{4,5},{5,4},{6,7},{7,6},{8,9},{9,8},{10,11... | collective-permute-start | bytes 1769480 | tf_op jit(solution)/shard_map/ppermute | solution.py:668
  50.0 22.6 %collective-permute-start.13 = (bf16[96,3072]{1,0:T(8,128)(2,1)}, bf16[96,3072]{1,0:T(8,128)(2,1)S(1)}, u32[]{:S(2)}, u32[]{:S(2)}) collective-permute-start(bf16[96,3072]{1,0:T(8,128)(2,1)} %collective-permute-done.6.refs_4_.refs_6_), channel_id=1, source_target_pairs={{0,2},{1,3},{2,0},{3,1},{4,6},{5,7},{6,4},{7,5},{8,10},{9,11},{10,... | collective-permute-start | bytes 1769480 | tf_op jit(solution)/shard_map/ppermute | solution.py:668
  60.0 15.2 %collective-permute-start.18 = (bf16[384,768]{1,0:T(8,128)(2,1)}, bf16[384,768]{1,0:T(8,128)(2,1)S(1)}, u32[]{:S(2)}, u32[]{:S(2)}) collective-permute-start(bf16[384,768]{1,0:T(8,128)(2,1)} %collective-permute-done.14.refs_13_), channel_id=1, source_target_pairs={{0,4},{1,5},{2,6},{3,7},{4,0},{5,1},{6,2},{7,3},{8,12},{9,13},{10,... | collective-permute-start | bytes 1769480 | tf_op jit(solution)/shard_map/ppermute | solution.py:668
  61.8 13.5 %collective-permute-start.19 = (bf16[384,768]{1,0:T(8,128)(2,1)}, bf16[384,768]{1,0:T(8,128)(2,1)S(1)}, u32[]{:S(2)}, u32[]{:S(2)}) collective-permute-start(bf16[384,768]{1,0:T(8,128)(2,1)} %collective-permute-done.14.refs_13_), channel_id=1, source_target_pairs={{0,1},{1,0},{2,3},{3,2},{4,5},{5,4},{6,7},{7,6},{8,9},{9,8},{10,11... | collective-permute-start | bytes 1769480 | tf_op jit(solution)/shard_map/ppermute | solution.py:668
  61.8 13.5 %collective-permute-start.20 = (bf16[384,768]{1,0:T(8,128)(2,1)}, bf16[384,768]{1,0:T(8,128)(2,1)S(1)}, u32[]{:S(2)}, u32[]{:S(2)}) collective-permute-start(bf16[384,768]{1,0:T(8,128)(2,1)} %collective-permute-done.15.refs_14_), channel_id=1, source_target_pairs={{0,1},{1,0},{2,3},{3,2},{4,5},{5,4},{6,7},{7,6},{8,9},{9,8},{10,11... | collective-permute-start | bytes 1769480 | tf_op jit(solution)/shard_map/ppermute | solution.py:668
  102.4 32.4 %collective-permute-start.24 = (bf16[4,384,768]{2,1,0:T(8,128)(2,1)}, bf16[4,384,768]{2,1,0:T(8,128)(2,1)}, u32[]{:S(2)}, u32[]{:S(2)}) collective-permute-start(bf16[4,384,768]{2,1,0:T(8,128)(2,1)} %get-tuple-element.136), channel_id=1, source_target_pairs={{0,1},{1,0},{2,3},{3,2},{4,5},{5,4},{6,7},{7,6},{8,9},{9,8},{10,11... | collective-permute-start | bytes 7077896 | tf_op jit(solution)/shard_map/ppermute | solution.py:668
  102.6 38.1 %collective-permute-start.25 = (bf16[4,384,768]{2,1,0:T(8,128)(2,1)}, bf16[4,384,768]{2,1,0:T(8,128)(2,1)}, u32[]{:S(2)}, u32[]{:S(2)}) collective-permute-start(bf16[4,384,768]{2,1,0:T(8,128)(2,1)} %get-tuple-element.141), channel_id=1, source_target_pairs={{0,1},{1,0},{2,3},{3,2},{4,5},{5,4},{6,7},{7,6},{8,9},{9,8},{10,11... | collective-permute-start | bytes 7077896 | tf_op jit(solution)/shard_map/ppermute | solution.py:668
  137.5 26.4 %collective-permute-start.28 = (bf16[2,192,768]{2,1,0:T(8,128)(2,1)}, bf16[2,192,768]{2,1,0:T(8,128)(2,1)}, u32[]{:S(2)}, u32[]{:S(2)}) collective-permute-start(bf16[2,192,768]{2,1,0:T(8,128)(2,1)} %get-tuple-element.186), channel_id=1, source_target_pairs={{0,2},{1,3},{2,0},{3,1},{4,6},{5,7},{6,4},{7,5},{8,10},{9,11},{10,... | collective-permute-start | bytes 1769480 | tf_op jit(solution)/shard_map/ppermute | solution.py:668
  139.1 24.8 %collective-permute-start.29 = (bf16[2,192,768]{2,1,0:T(8,128)(2,1)}, bf16[2,192,768]{2,1,0:T(8,128)(2,1)}, u32[]{:S(2)}, u32[]{:S(2)}) collective-permute-start(bf16[2,192,768]{2,1,0:T(8,128)(2,1)} %get-tuple-element.185), channel_id=1, source_target_pairs={{0,4},{1,5},{2,6},{3,7},{4,0},{5,1},{6,2},{7,3},{8,12},{9,13},{10,... | collective-permute-start | bytes 1769480 | tf_op jit(solution)/shard_map/ppermute | solution.py:668
  146.3 22.2 %collective-permute-start.26 = (bf16[2,48,3200]{2,1,0:T(8,128)(2,1)}, bf16[2,48,3200]{2,1,0:T(8,128)(2,1)}, u32[]{:S(2)}, u32[]{:S(2)}) collective-permute-start(bf16[2,48,3200]{2,1,0:T(8,128)(2,1)} %get-tuple-element.182), channel_id=1, source_target_pairs={{0,2},{1,3},{2,0},{3,1},{4,6},{5,7},{6,4},{7,5},{8,10},{9,11},{10,... | collective-permute-start | bytes 1843208 | tf_op jit(solution)/shard_map/ppermute | solution.py:668
  146.8 21.8 %collective-permute-start.27 = (bf16[2,48,3200]{2,1,0:T(8,128)(2,1)}, bf16[2,48,3200]{2,1,0:T(8,128)(2,1)}, u32[]{:S(2)}, u32[]{:S(2)}) collective-permute-start(bf16[2,48,3200]{2,1,0:T(8,128)(2,1)} %get-tuple-element.181), channel_id=1, source_target_pairs={{0,4},{1,5},{2,6},{3,7},{4,0},{5,1},{6,2},{7,3},{8,12},{9,13},{10,... | collective-permute-start | bytes 1843208 | tf_op jit(solution)/shard_map/ppermute | solution.py:668
  147.1 31.1 %collective-permute-start.34 = (bf16[4,192,768]{2,1,0:T(8,128)(2,1)}, bf16[4,192,768]{2,1,0:T(8,128)(2,1)S(1)}, u32[]{:S(2)}, u32[]{:S(2)}) collective-permute-start(bf16[4,192,768]{2,1,0:T(8,128)(2,1)} %add_convert_fusion), channel_id=1, source_target_pairs={{0,8},{8,0},{16,24},{24,16},{1,9},{9,1},{17,25},{25,17},{2,10},{10... | collective-permute-start | bytes 3538952 | tf_op jit(solution)/shard_map/ppermute | solution.py:770
  170.1 11.5 %collective-permute-start.30 = (bf16[48,3200]{1,0:T(8,128)(2,1)S(1)}, bf16[48,3200]{1,0:T(8,128)(2,1)S(1)}, u32[]{:S(2)}, u32[]{:S(2)}) collective-permute-start(bf16[48,3200]{1,0:T(8,128)(2,1)S(1)} %get-tuple-element.180), channel_id=1, source_target_pairs={{0,4},{1,5},{2,6},{3,7},{4,0},{5,1},{6,2},{7,3},{8,12},{9,13},{10,... | collective-permute-start | bytes 921608 | tf_op jit(solution)/shard_map/ppermute | solution.py:668
  171.7 10.4 %collective-permute-start.31 = (bf16[48,3200]{1,0:T(8,128)(2,1)S(1)}, bf16[48,3200]{1,0:T(8,128)(2,1)S(1)}, u32[]{:S(2)}, u32[]{:S(2)}) collective-permute-start(bf16[48,3200]{1,0:T(8,128)(2,1)S(1)} %get-tuple-element.179), channel_id=1, source_target_pairs={{0,2},{1,3},{2,0},{3,1},{4,6},{5,7},{6,4},{7,5},{8,10},{9,11},{10,... | collective-permute-start | bytes 921608 | tf_op jit(solution)/shard_map/ppermute | solution.py:668
  179.7 23.0 %collective-permute-start.37 = (bf16[2,192,768]{2,1,0:T(8,128)(2,1)S(1)}, bf16[2,192,768]{2,1,0:T(8,128)(2,1)S(1)}, u32[]{:S(2)}, u32[]{:S(2)}) collective-permute-start(bf16[2,192,768]{2,1,0:T(8,128)(2,1)S(1)} %add_convert_fusion.3), channel_id=1, source_target_pairs={{0,2},{1,3},{2,0},{3,1},{4,6},{5,7},{6,4},{7,5},{8,10},{9,11},{10,... | collective-permute-start | bytes 1769480 | tf_op jit(solution)/shard_map/ppermute | solution.py:668
  184.0 14.5 %collective-permute-start.35 = (bf16[48,3200]{1,0:T(8,128)(2,1)S(1)}, bf16[48,3200]{1,0:T(8,128)(2,1)S(1)}, u32[]{:S(2)}, u32[]{:S(2)}) collective-permute-start(bf16[48,3200]{1,0:T(8,128)(2,1)S(1)} %select_convert_fusion), channel_id=1, source_target_pairs={{0,8},{8,0},{16,24},{24,16},{1,9},{9,1},{17,25},{25,17},{2,10},{10... | collective-permute-start | bytes 921608 | tf_op jit(solution)/shard_map/ppermute | solution.py:736
  187.1 18.3 %collective-permute-start.38 = (bf16[192,768]{1,0:T(8,128)(2,1)S(1)}, bf16[192,768]{1,0:T(8,128)(2,1)S(1)}, u32[]{:S(2)}, u32[]{:S(2)}) collective-permute-start(bf16[192,768]{1,0:T(8,128)(2,1)S(1)} %add_convert_fusion.13), channel_id=1, source_target_pairs={{0,24},{24,0},{8,16},{16,8},{1,25},{25,1},{9,17},{17,9},{2,26},{26... | collective-permute-start | bytes 884744 | tf_op jit(solution)/shard_map/ppermute | solution.py:743
  200.1 15.6 %collective-permute-start.39 = (bf16[48,3200]{1,0:T(8,128)(2,1)S(1)}, bf16[48,3200]{1,0:T(8,128)(2,1)S(1)}, u32[]{:S(2)}, u32[]{:S(2)}) collective-permute-start(bf16[48,3200]{1,0:T(8,128)(2,1)S(1)} %add_convert_fusion.7), channel_id=1, source_target_pairs={{0,24},{24,0},{8,16},{16,8},{1,25},{25,1},{9,17},{17,9},{2,26},{26... | collective-permute-start | bytes 921608 | tf_op jit(solution)/shard_map/ppermute | solution.py:743
  205.5 14.4 %collective-permute-start.44 = (bf16[192,768]{1,0:T(8,128)(2,1)S(1)}, bf16[192,768]{1,0:T(8,128)(2,1)S(1)}, u32[]{:S(2)}, u32[]{:S(2)}) collective-permute-start(bf16[192,768]{1,0:T(8,128)(2,1)S(1)} %add_convert_fusion.11), channel_id=1, source_target_pairs={{0,8},{8,0},{16,24},{24,16},{1,9},{9,1},{17,25},{25,17},{2,10},{10... | collective-permute-start | bytes 884744 | tf_op jit(solution)/shard_map/ppermute | solution.py:749
  211.8 12.7 %collective-permute-start.42 = (bf16[192,768]{1,0:T(8,128)(2,1)S(1)}, bf16[192,768]{1,0:T(8,128)(2,1)S(1)}, u32[]{:S(2)}, u32[]{:S(2)}) collective-permute-start(bf16[192,768]{1,0:T(8,128)(2,1)S(1)} %fusion.2), channel_id=1, source_target_pairs={{0,24},{24,0},{8,16},{16,8},{1,25},{25,1},{9,17},{17,9},{2,26},{26... | collective-permute-start | bytes 884744 | tf_op jit(solution)/shard_map/ppermute | solution.py:790
  215.8 11.8 %collective-permute-start.41 = (bf16[48,3200]{1,0:T(8,128)(2,1)S(1)}, bf16[48,3200]{1,0:T(8,128)(2,1)S(1)}, u32[]{:S(2)}, u32[]{:S(2)}) collective-permute-start(bf16[48,3200]{1,0:T(8,128)(2,1)S(1)} %add_convert_fusion.6), channel_id=1, source_target_pairs={{0,8},{8,0},{16,24},{24,16},{1,9},{9,1},{17,25},{25,17},{2,10},{10... | collective-permute-start | bytes 921608 | tf_op jit(solution)/shard_map/ppermute | solution.py:749
  (69 other events, 672.8 us)
